TPU v7x, 32 devices: a whole 2x2x4 slice. The times are simulated.
32 devices in a mesh: fold: 4 (over x, core), blk: 8 (over z, y).
Axes of the slice: x: 2, y: 2, z: 4, core: 2. Of those that a mesh axis runs over, the one named last changes fastest.
Arguments:
- fine_rhs: float32 [1536, 32, 128], P(('fold', 'blk')), may hold values from -6 to 6
- fine_tiles: bfloat16 [1536, 5, 128, 128], P(('fold', 'blk')), as said below
- fine_cols: int32 [1536, 5], P(('fold', 'blk')), may hold values from 0 to 1535, as said below
- fine_smoother: bfloat16 [1536, 128, 128], P(('fold', 'blk'))
- fine_map: int32 [1536], P(('fold', 'blk')), may hold values from 0 to 383, as said below
- fine_slots: int32 [1536, 128], P(('fold', 'blk')), may hold values from 0 to 127
- mid_tiles: bfloat16 [384, 5, 128, 128], P(('fold', 'blk'))
- mid_cols: int32 [384, 5], P(('fold', 'blk')), may hold values from 0 to 383, as said below
- mid_smoother: bfloat16 [384, 128, 128], P(('fold', 'blk'))
- mid_map: int32 [384], P(('fold', 'blk')), may hold values from 0 to 95, as said below
- mid_slots: int32 [384, 128], P(('fold', 'blk')), may hold values from 0 to 127
- coarse_tiles: bfloat16 [96, 5, 128, 128], P('blk')
- coarse_cols: int32 [96, 5], P('blk'), may hold values from 0 to 95, as said below
- coarse_smoother: bfloat16 [96, 128, 128], P('blk')
Outputs:
- fine_field: float32 [1536, 32, 128], P(('fold', 'blk'))
- mid_field: float32 [384, 32, 128], P(('fold', 'blk'))
- coarse_field: float32 [96, 32, 128], P('blk')
Inputs may be any that keep to these rules, and one draw needn't show every extreme that they name: `fine_cols`: column 0 of each row names the row's own block; every other entry names a level-0 block of a device with the same fold index whose blk index differs by at most one, cyclically. `mid_cols`: column 0 of each row names the row's own block; every other entry names a level-1 block of a device with the same fold index whose blk index differs by at most one, cyclically. `coarse_cols`: column 0 of each row names the row's own block; every other entry names a level-2 block whose blk index differs from the row's by at most one, cyclically. `fine_map`: A level-0 block's level-1 block lies on a device with the same fold index; of the level-0 blocks of one device at most 12 have their level-1 blocks on any one device, and in every fold row some device receives exactly 12 from every device of that row. `mid_map`: A level-1 block's level-2 block lies at the same blk index. `fine_tiles`: each smoother tile is close to half the inverse of the diagonal of the row block's diagonal tile.
All inputs are finite; a program needn't handle non-finite values.
Results may differ from a plain program's by a relative error of at most 0.012.
Values may be sent and summed in bfloat16 or wider, within the bound.
No kernel may reach another device: no remote copies, remote signals or barrier semaphores. Data moves between devices by JAX's collectives and lax.ppermute only.
A program may use at most 128 MiB of HBM per device.

v0:
```python
import jax
import jax.numpy as jnp
from jax import lax
from jax.sharding import PartitionSpec as P

VB = 128
R = 32
COARSE = 8


def extended(value, sides, width):
    for axis, dim in sides:
        size, length = (lax.axis_size(axis), value.shape[dim])
        up = [(i, (i + 1) % size) for i in range(size)]
        down = [(j, i) for i, j in up]
        last = lax.slice_in_dim(value, length - width, length, axis=dim)
        first = lax.slice_in_dim(value, 0, width, axis=dim)
        before = lax.ppermute(last, axis, up)
        after = lax.ppermute(first, axis, down)
        value = jnp.concatenate([before, value, after], axis=dim)
    return value


def apply_tiles(tiles, columns, rough):
    per_device = rough.shape[0]
    blk_count = lax.axis_size("blk")
    widened = extended(rough, (("blk", 0),), per_device)
    my_blk = lax.axis_index("blk")
    owner = columns // per_device % blk_count
    offset = (owner - my_blk + 1 + blk_count) % blk_count
    local_index = offset * per_device + columns % per_device
    chooser = (
        local_index[:, :, None] == jnp.arange(widened.shape[0], dtype=jnp.int32)[None, None, :]
    ).astype(jnp.bfloat16)
    picked = jnp.einsum(
        "ikj,jrw->ikrw", chooser, widened, preferred_element_type=jnp.float32
    ).astype(jnp.bfloat16)
    return jnp.einsum("ikuw,ikrw->iru", tiles, picked, preferred_element_type=jnp.float32)


def smooth_tiles(smoother, resid):
    return jnp.einsum(
        "iuw,irw->iru", smoother, resid.astype(jnp.bfloat16), preferred_element_type=jnp.float32
    )


def sweep_level(tiles, columns, smoother, rhs_field, field):
    return field + smooth_tiles(
        smoother, rhs_field - apply_tiles(tiles, columns, field.astype(jnp.bfloat16))
    )


def slot_table(slots):
    return (slots[:, :, None] == jnp.arange(VB, dtype=jnp.int32)[None, None, :]).astype(jnp.float32)


def collect_slots(field, table):
    return jnp.einsum("jrv,jvs->jrs", field, table, precision=lax.Precision.HIGHEST)


def spread_slots(coarse, table):
    return jnp.einsum("jrs,jvs->jrv", coarse, table, precision=lax.Precision.HIGHEST)


def on_device(
    fine_rhs,
    fine_tiles,
    fine_cols,
    fine_smoother,
    fine_map,
    fine_slots,
    mid_tiles,
    mid_cols,
    mid_smoother,
    mid_map,
    mid_slots,
    coarse_tiles,
    coarse_cols,
    coarse_smoother,
):
    fine_count = fine_rhs.shape[0]
    mid_count = mid_tiles.shape[0]
    low_count = coarse_tiles.shape[0]
    blk_count = lax.axis_size("blk")
    fine_table = slot_table(fine_slots)
    mid_table = slot_table(mid_slots)
    fine_pre = smooth_tiles(fine_smoother, fine_rhs)
    fine_pre = sweep_level(fine_tiles, fine_cols, fine_smoother, fine_rhs, fine_pre)
    fine_resid = fine_rhs - apply_tiles(fine_tiles, fine_cols, fine_pre.astype(jnp.bfloat16))
    pieces = collect_slots(fine_resid, fine_table)
    destination = fine_map // mid_count % blk_count
    target = fine_map % mid_count
    capacity = max(2, 2 * fine_count // blk_count)
    same_dest = destination[:, None] == destination[None, :]
    earlier = jnp.arange(fine_count)[None, :] < jnp.arange(fine_count)[:, None]
    rank_index = jnp.sum(same_dest & earlier, axis=1)
    slot_index = destination * capacity + rank_index
    routing = jnp.arange(blk_count * capacity, dtype=jnp.int32)[:, None] == slot_index[None, :]
    routing_float = routing.astype(jnp.float32)
    send_rows = jnp.einsum(
        "qj,jrs->qrs", routing_float, pieces, precision=lax.Precision.HIGHEST
    ).reshape(blk_count, capacity, R, VB)
    send_target = (jnp.sum(jnp.where(routing, target[None, :] + 1, 0), axis=1) - 1).reshape(
        blk_count, capacity
    )
    received, received_target = (
        lax.all_to_all(send_rows, "blk", split_axis=0, concat_axis=0, tiled=True),
        lax.all_to_all(send_target, "blk", split_axis=0, concat_axis=0, tiled=True),
    )
    flat_target = received_target.reshape(-1)
    landing = (flat_target[None, :] == jnp.arange(mid_count, dtype=jnp.int32)[:, None]).astype(
        jnp.float32
    )
    mid_rhs = jnp.einsum(
        "tq,qrs->trs", landing, received.reshape(-1, R, VB), precision=lax.Precision.HIGHEST
    )
    mid_pre = smooth_tiles(mid_smoother, mid_rhs)
    mid_pre = sweep_level(mid_tiles, mid_cols, mid_smoother, mid_rhs, mid_pre)
    mid_resid = mid_rhs - apply_tiles(mid_tiles, mid_cols, mid_pre.astype(jnp.bfloat16))
    low_index = mid_map % low_count
    low_pick = (jnp.arange(low_count, dtype=jnp.int32)[:, None] == low_index[None, :]).astype(
        jnp.float32
    )
    low_terms = jnp.einsum(
        "tj,jrs->trs",
        low_pick,
        collect_slots(mid_resid, mid_table),
        precision=lax.Precision.HIGHEST,
    )
    coarse_rhs = lax.psum(low_terms.astype(jnp.bfloat16), "fold").astype(jnp.float32)
    coarse_field = smooth_tiles(coarse_smoother, coarse_rhs)

    def full_sweep(sweep_turn, field):
        return sweep_level(coarse_tiles, coarse_cols, coarse_smoother, coarse_rhs, field)

    coarse_field = lax.fori_loop(0, COARSE - 1, full_sweep, coarse_field)
    lifted = jnp.einsum("tj,trs->jrs", low_pick, coarse_field, precision=lax.Precision.HIGHEST)
    mid_field = mid_pre + spread_slots(lifted, mid_table)
    mid_field = sweep_level(mid_tiles, mid_cols, mid_smoother, mid_rhs, mid_field)
    answers = jnp.einsum(
        "tq,trs->qrs", landing, mid_field, precision=lax.Precision.HIGHEST
    ).reshape(blk_count, capacity, R, VB)
    returned = lax.all_to_all(
        answers.astype(jnp.bfloat16), "blk", split_axis=0, concat_axis=0, tiled=True
    ).astype(answers.dtype)
    fine_coarse = jnp.einsum(
        "qj,qrs->jrs", routing_float, returned.reshape(-1, R, VB), precision=lax.Precision.HIGHEST
    )
    fine_field = fine_pre + spread_slots(fine_coarse, fine_table)
    fine_field = sweep_level(fine_tiles, fine_cols, fine_smoother, fine_rhs, fine_field)
    return (fine_field, mid_field, coarse_field)


def solution(mesh):
    placed = (
        P(("fold", "blk"), None, None),
        P(("fold", "blk"), None, None, None),
        P(("fold", "blk"), None),
        P(("fold", "blk"), None, None),
        P(("fold", "blk")),
        P(("fold", "blk"), None),
        P(("fold", "blk"), None, None, None),
        P(("fold", "blk"), None),
        P(("fold", "blk"), None, None),
        P(("fold", "blk")),
        P(("fold", "blk"), None),
        P("blk", None, None, None),
        P("blk", None),
        P("blk", None, None),
    )
    return jax.shard_map(
        on_device,
        mesh=mesh,
        in_specs=placed,
        out_specs=(
            P(("fold", "blk"), None, None),
            P(("fold", "blk"), None, None),
            P("blk", None, None),
        ),
        check_vma=False,
    )
```

profile of v0, /device:TPU:0, one launch (start us, length us, event | category | flops | bytes accessed | tf_op | source)
XLA Modules:
  0.0 333.7 jit_solution(11358576831007558513)
XLA Ops:
  7.2 3.6 %fusion.147 = (bf16[48,32,128]{2,1,0:T(8,128)(2,1)S(1)}, f32[48,32,128]{2,1,0:T(8,128)}) fusion(bf16[48,128,128]{2,1,0:T(8,128)(2,1)} %param.19, f32[48,32,128]{2,1,0:T(8,128)} %param.16), kind=kOutput, calls=%fused_computation.184 | convolution fusion | flops 50724864 | bytes 3538944 | tf_op jit(solution)/shard_map/iuw,irw->iru/dot_general | solution.py:42
  10.8 6.0 %collective-permute-start.3 = (bf16[48,32,128]{2,1,0:T(8,128)(2,1)S(1)}, bf16[48,32,128]{2,1,0:T(8,128)(2,1)S(1)}, u32[]{:S(2)}, u32[]{:S(2)}) collective-permute-start(bf16[48,32,128]{2,1,0:T(8,128)(2,1)S(1)} %get-tuple-element.203), channel_id=1, source_target_pairs={{1,0},{2,1},{3,2},{4,3},{5,4},{6,5},{7,6},{0,7},{9,8},{10,9},{11,1... | collective-permute-start | bytes 1179656 | tf_op jit(solution)/shard_map/ppermute | solution.py:19
  17.0 14.3 %collective-permute-done.3 = bf16[48,32,128]{2,1,0:T(8,128)(2,1)S(1)} collective-permute-done((bf16[48,32,128]{2,1,0:T(8,128)(2,1)S(1)}, bf16[48,32,128]{2,1,0:T(8,128)(2,1)S(1)}, u32[]{:S(2)}, u32[]{:S(2)}) %collective-permute-start.3) | collective-permute-done | bytes 393248 | tf_op jit(solution)/shard_map/ppermute | solution.py:19
  33.7 8.8 %fusion.148 = (bf16[48,32,128]{2,1,0:T(8,128)(2,1)}, f32[48,32,128]{2,1,0:T(8,128)}) fusion(f32[48,32,128]{2,1,0:T(8,128)} %get-tuple-element.204, bf16[48,128,128]{2,1,0:T(8,128)(2,1)S(1)} %copy-done.1, f32[48,32,128]{2,1,0:T(8,128)} %param.16, bf16[48,5,128,128]{3,2,1,0:T(8,128)(2,1)} %param.17, bf16[48,5,32,128]{3,0,2,1:T(8,128)(2,1)} %convolution_convert_fusion.3), kind=kOutput, calls=%fused_computation.185 | convolution fusion | flops 302776320 | bytes 14155776 | tf_op jit(solution)/shard_map/iuw,irw->iru/dot_general | solution.py:42
  42.5 4.9 %collective-permute-start.5 = (bf16[48,32,128]{2,1,0:T(8,128)(2,1)}, bf16[48,32,128]{2,1,0:T(8,128)(2,1)S(1)}, u32[]{:S(2)}, u32[]{:S(2)}) collective-permute-start(bf16[48,32,128]{2,1,0:T(8,128)(2,1)} %get-tuple-element.205), channel_id=1, source_target_pairs={{1,0},{2,1},{3,2},{4,3},{5,4},{6,5},{7,6},{0,7},{9,8},{10,9},{11,1... | collective-permute-start | bytes 1179656 | tf_op jit(solution)/shard_map/ppermute | solution.py:19
  48.2 6.0 %all-to-all-start = ((s32[8,1,12]{2,1,0:T(1,128)}), s32[8,1,12]{2,1,0:T(1,128)S(1)}, u32[]{:S(2)}, u32[]{:S(2)}) async-start(s32[8,1,12]{2,1,0:T(1,128)} %bitcast.12), calls=%async_computation | async-start | bytes 8192 | tf_op jit(solution)/shard_map/all_to_all | solution.py:108
  54.2 8.8 %collective-permute-done.5 = bf16[48,32,128]{2,1,0:T(8,128)(2,1)S(1)} collective-permute-done((bf16[48,32,128]{2,1,0:T(8,128)(2,1)}, bf16[48,32,128]{2,1,0:T(8,128)(2,1)S(1)}, u32[]{:S(2)}, u32[]{:S(2)}) %collective-permute-start.5) | collective-permute-done | bytes 393248 | tf_op jit(solution)/shard_map/ppermute | solution.py:19
  65.5 5.0 %fusion.40 = f32[48,32,128]{2,1,0:T(8,128)S(1)} fusion(f32[48,32,128]{2,1,0:T(8,128)S(1)} %copy-done.4, bf16[48,5,128,128]{3,2,1,0:T(8,128)(2,1)} %param.17, bf16[48,5,32,128]{3,0,2,1:T(8,128)(2,1)S(1)} %convolution_convert_fusion.2), kind=kOutput, calls=%fused_computation.56 | convolution fusion | flops 251854848 | bytes 11403264 | tf_op jit(solution)/shard_map/ikuw,ikrw->iru/dot_general | solution.py:38
  76.8 4.3 %all-to-all-start.1 = ((f32[8,12,32,128]{3,2,1,0:T(8,128)}), f32[8,12,32,128]{3,2,1,0:T(8,128)S(1)}, u32[]{:S(2)}, u32[]{:S(2)}) async-start(f32[8,12,32,128]{3,2,1,0:T(8,128)} %bitcast.158), calls=%async_computation.1 | async-start | bytes 3145728 | tf_op jit(solution)/shard_map/all_to_all | solution.py:107
  82.4 35.3 %all-to-all-done.1 = f32[8,12,32,128]{3,2,1,0:T(8,128)S(1)} async-done(((f32[8,12,32,128]{3,2,1,0:T(8,128)}), f32[8,12,32,128]{3,2,1,0:T(8,128)S(1)}, u32[]{:S(2)}, u32[]{:S(2)}) %all-to-all-start.1) | async-done | bytes 1572896 | tf_op jit(solution)/shard_map/all_to_all | solution.py:107
  124.9 5.1 %collective-permute-done.6 = bf16[12,32,128]{2,1,0:T(8,128)(2,1)S(1)} collective-permute-done((bf16[12,32,128]{2,1,0:T(8,128)(2,1)S(1)}, bf16[12,32,128]{2,1,0:T(8,128)(2,1)S(1)}, u32[]{:S(2)}, u32[]{:S(2)}) %collective-permute-start.6) | collective-permute-done | bytes 98336 | tf_op jit(solution)/shard_map/ppermute | solution.py:18
  134.2 3.6 %collective-permute-done.9 = bf16[12,32,128]{2,1,0:T(8,128)(2,1)S(1)} collective-permute-done((bf16[12,32,128]{2,1,0:T(8,128)(2,1)}, bf16[12,32,128]{2,1,0:T(8,128)(2,1)S(1)}, u32[]{:S(2)}, u32[]{:S(2)}) %collective-permute-start.9) | collective-permute-done | bytes 98336 | tf_op jit(solution)/shard_map/ppermute | solution.py:19
  143.6 28.8 %all-reduce.2.cloned.1.call-done = bf16[12,32,128]{2,0,1:T(8,128)(2,1)} async-done(((bf16[12,32,128]{2,0,1:T(8,128)(2,1)}), bf16[12,32,128]{2,0,1:T(8,128)(2,1)}) %all-reduce.2.cloned.1.call-update) | async-done | bytes 98320 | tf_op jit(solution)/shard_map/psum | solution.py:130
  175.4 87.6 %while.13 = (s32[]{:T(128)}, f32[12,32,128]{2,0,1:T(8,128)S(1)}, s32[12,5,1]{0,1,2:T(8,128)S(1)}, s32[12,5]{0,1:T(8,128)S(1)}, bf16[12,5,128,128]{3,2,1,0:T(8,12...) while((s32[]{:T(128)}, f32[12,32,128]{2,0,1:T(8,128)S(1)}, ...), condition=%wide.region_4.5_spmd, body=%wide.region_3.4_spmd.sunk | while | flops 94523680 | bytes 6096033 | solution.py:136
  176.9 3.2 collective-permute-start
  180.2 3.0 collective-permute-done.1
  189.4 3.3 collective-permute-start
  192.7 3.0 collective-permute-done.1
  201.9 3.3 collective-permute-start
  205.3 3.0 collective-permute-done.1
  214.4 3.3 collective-permute-start
  217.8 3.0 collective-permute-done.1
  227.0 3.3 collective-permute-start
  239.5 3.3 collective-permute-start
  242.9 3.0 collective-permute-done.1
  251.1 4.3 %collective-permute-start = (bf16[12,32,128]{2,0,1:T(8,128)(2,1)S(1)}, bf16[12,32,128]{2,0,1:T(8,128)(2,1)}, u32[]{:S(2)}, u32[]{:S(2)}) collective-permute-start(bf16[12,32,128]{2,0,1:T(8,128)(2,1)S(1)} %convert_element_type.172), channel_id=1, source_target_pairs={{1,0},{2,1},{3,2},{4,3},{5,4},{6,5},{7,6},{0,7},{9,8},{10,9},{11,1... | collective-permute-start | bytes 294920 | tf_op jit(solution)/shard_map/while/body/eval_jaxpr/ppermute | solution.py:19
  265.8 4.2 %collective-permute-start.11 = (bf16[12,32,128]{2,1,0:T(8,128)(2,1)S(1)}, bf16[12,32,128]{2,1,0:T(8,128)(2,1)S(1)}, u32[]{:S(2)}, u32[]{:S(2)}) collective-permute-start(bf16[12,32,128]{2,1,0:T(8,128)(2,1)S(1)} %get-tuple-element.213), channel_id=1, source_target_pairs={{1,0},{2,1},{3,2},{4,3},{5,4},{6,5},{7,6},{0,7},{9,8},{10,9},{11,1... | collective-permute-start | bytes 294920 | tf_op jit(solution)/shard_map/ppermute | solution.py:19
  272.2 5.1 %collective-permute-done.10 = bf16[12,32,128]{2,1,0:T(8,128)(2,1)S(1)} collective-permute-done((bf16[12,32,128]{2,1,0:T(8,128)(2,1)S(1)}, bf16[12,32,128]{2,1,0:T(8,128)(2,1)S(1)}, u32[]{:S(2)}, u32[]{:S(2)}) %collective-permute-start.10) | collective-permute-done | bytes 98336 | tf_op jit(solution)/shard_map/ppermute | solution.py:18
  282.4 17.1 %all_to_all.16 = bf16[8,12,32,128]{3,2,1,0:T(8,128)(2,1)S(1)} all-to-all(bf16[8,12,32,128]{3,2,1,0:T(8,128)(2,1)S(1)} %bitcast.160), channel_id=1, replica_groups=mesh['fold'=4,'blk'=8] {'blk'}, dimensions={0} | all-to-all | bytes 1572864 | tf_op jit(solution)/shard_map/all_to_all | solution.py:143
  299.9 3.9 %fusion.157 = (bf16[48,32,128]{2,1,0:T(8,128)(2,1)S(1)}, f32[48,32,128]{2,1,0:T(8,128)}) fusion(f32[48,32,128]{2,1,0:T(8,128)S(1)} %copy-done.9, s32[48,128]{1,0:T(8,128)S(1)} %copy-done.14, f32[48,32,128]{2,0,1:T(8,128)S(1)} %fusion.71), kind=kOutput, calls=%fused_computation.190 | convolution fusion | flops 303169536 | bytes 2777088 | tf_op jit(solution)/shard_map/jrs,jvs->jrv/dot_general | solution.py:62
  306.7 9.2 %collective-permute-done.13 = bf16[48,32,128]{2,1,0:T(8,128)(2,1)S(1)} collective-permute-done((bf16[48,32,128]{2,1,0:T(8,128)(2,1)S(1)}, bf16[48,32,128]{2,1,0:T(8,128)(2,1)S(1)}, u32[]{:S(2)}, u32[]{:S(2)}) %collective-permute-start.13) | collective-permute-done | bytes 393248 | tf_op jit(solution)/shard_map/ppermute | solution.py:19
  318.2 8.7 %convolution_add_fusion.1 = f32[48,32,128]{2,1,0:T(8,128)} fusion(f32[48,32,128]{2,1,0:T(8,128)} %get-tuple-element.216, bf16[48,128,128]{2,1,0:T(8,128)(2,1)S(1)} %copy-done.2, f32[48,32,128]{2,1,0:T(8,128)} %param.16, bf16[48,5,128,128]{3,2,1,0:T(8,128)(2,1)} %param.17, bf16[48,5,32,128]{3,0,2,1:T(8,128)(2,1)} %convolution_convert_fusion.1), kind=kOutput, calls=%fused_computation.51 | convolution fusion | flops 302579712 | bytes 13762560 | tf_op jit(solution)/shard_map/iuw,irw->iru/dot_general | solution.py:42
  (167 shorter events, 97.1 us)
Async XLA Ops:
  7.2 123.2 %copy-start = (bf16[12,5,128,128]{3,2,1,0:T(8,128)(2,1)S(1)}, bf16[12,5,128,128]{3,2,1,0:T(8,128)(2,1)}, u32[]{:S(2)}) copy-start(bf16[12,5,128,128]{3,2,1,0:T(8,128)(2,1)} %param.22) | copy-start | bytes 5898244
  10.8 20.5 %collective-permute-start.3 = (bf16[48,32,128]{2,1,0:T(8,128)(2,1)S(1)}, bf16[48,32,128]{2,1,0:T(8,128)(2,1)S(1)}, u32[]{:S(2)}, u32[]{:S(2)}) collective-permute-start(bf16[48,32,128]{2,1,0:T(8,128)(2,1)S(1)} %get-tuple-element.203), channel_id=1, source_target_pairs={{1,0},{2,1},{3,2},{4,3},{5,4},{6,5},{7,6},{0,7},{9,8},{10,9},{11,1... | collective-permute-start | bytes 1179656 | tf_op jit(solution)/shard_map/ppermute | solution.py:19
  16.8 14.7 %collective-permute-start.2 = (bf16[48,32,128]{2,1,0:T(8,128)(2,1)S(1)}, bf16[48,32,128]{2,1,0:T(8,128)(2,1)S(1)}, u32[]{:S(2)}, u32[]{:S(2)}) collective-permute-start(bf16[48,32,128]{2,1,0:T(8,128)(2,1)S(1)} %get-tuple-element.203), channel_id=1, source_target_pairs={{0,1},{1,2},{2,3},{3,4},{4,5},{5,6},{6,7},{7,0},{8,9},{9,10},{10,1... | collective-permute-start | bytes 1179656 | tf_op jit(solution)/shard_map/ppermute | solution.py:18
  42.5 20.5 %collective-permute-start.5 = (bf16[48,32,128]{2,1,0:T(8,128)(2,1)}, bf16[48,32,128]{2,1,0:T(8,128)(2,1)S(1)}, u32[]{:S(2)}, u32[]{:S(2)}) collective-permute-start(bf16[48,32,128]{2,1,0:T(8,128)(2,1)} %get-tuple-element.205), channel_id=1, source_target_pairs={{1,0},{2,1},{3,2},{4,3},{5,4},{6,5},{7,6},{0,7},{9,8},{10,9},{11,1... | collective-permute-start | bytes 1179656 | tf_op jit(solution)/shard_map/ppermute | solution.py:19
  47.4 15.9 %collective-permute-start.4 = (bf16[48,32,128]{2,1,0:T(8,128)(2,1)}, bf16[48,32,128]{2,1,0:T(8,128)(2,1)S(1)}, u32[]{:S(2)}, u32[]{:S(2)}) collective-permute-start(bf16[48,32,128]{2,1,0:T(8,128)(2,1)} %get-tuple-element.205), channel_id=1, source_target_pairs={{0,1},{1,2},{2,3},{3,4},{4,5},{5,6},{6,7},{7,0},{8,9},{9,10},{10,1... | collective-permute-start | bytes 1179656 | tf_op jit(solution)/shard_map/ppermute | solution.py:18
  47.4 26.0 %copy-start.17 = (s32[48]{0:T(128)}, s32[48]{0:T(128)S(1)}, u32[]{:S(2)}) copy-start(s32[48]{0:T(128)S(1)} %multiply_add_fusion) | copy-start | bytes 580
  48.2 28.6 %all-to-all-start = ((s32[8,1,12]{2,1,0:T(1,128)}), s32[8,1,12]{2,1,0:T(1,128)S(1)}, u32[]{:S(2)}, u32[]{:S(2)}) async-start(s32[8,1,12]{2,1,0:T(1,128)} %bitcast.12), calls=%async_computation | async-start | bytes 8192 | tf_op jit(solution)/shard_map/all_to_all | solution.py:108
  76.8 41.0 %all-to-all-start.1 = ((f32[8,12,32,128]{3,2,1,0:T(8,128)}), f32[8,12,32,128]{3,2,1,0:T(8,128)S(1)}, u32[]{:S(2)}, u32[]{:S(2)}) async-start(f32[8,12,32,128]{3,2,1,0:T(8,128)} %bitcast.158), calls=%async_computation.1 | async-start | bytes 3145728 | tf_op jit(solution)/shard_map/all_to_all | solution.py:107
  81.1 91.3 %all-reduce.2.cloned.1.call-start = ((), (), s32[]{:S(2)}) async-start(), calls=%async_computation.3 | async-start | bytes 262144 | tf_op jit(solution)/shard_map/psum | solution.py:130
  120.3 4.6 %collective-permute-start.7 = (bf16[12,32,128]{2,1,0:T(8,128)(2,1)S(1)}, bf16[12,32,128]{2,1,0:T(8,128)(2,1)S(1)}, u32[]{:S(2)}, u32[]{:S(2)}) collective-permute-start(bf16[12,32,128]{2,1,0:T(8,128)(2,1)S(1)} %get-tuple-element.209), channel_id=1, source_target_pairs={{1,0},{2,1},{3,2},{4,3},{5,4},{6,5},{7,6},{0,7},{9,8},{10,9},{11,1... | collective-permute-start | bytes 294920 | tf_op jit(solution)/shard_map/ppermute | solution.py:19
  122.6 7.3 %collective-permute-start.6 = (bf16[12,32,128]{2,1,0:T(8,128)(2,1)S(1)}, bf16[12,32,128]{2,1,0:T(8,128)(2,1)S(1)}, u32[]{:S(2)}, u32[]{:S(2)}) collective-permute-start(bf16[12,32,128]{2,1,0:T(8,128)(2,1)S(1)} %get-tuple-element.209), channel_id=1, source_target_pairs={{0,1},{1,2},{2,3},{3,4},{4,5},{5,6},{6,7},{7,0},{8,9},{9,10},{10,1... | collective-permute-start | bytes 294920 | tf_op jit(solution)/shard_map/ppermute | solution.py:18
  132.1 5.6 %collective-permute-start.9 = (bf16[12,32,128]{2,1,0:T(8,128)(2,1)}, bf16[12,32,128]{2,1,0:T(8,128)(2,1)S(1)}, u32[]{:S(2)}, u32[]{:S(2)}) collective-permute-start(bf16[12,32,128]{2,1,0:T(8,128)(2,1)} %get-tuple-element.211), channel_id=1, source_target_pairs={{1,0},{2,1},{3,2},{4,3},{5,4},{6,5},{7,6},{0,7},{9,8},{10,9},{11,1... | collective-permute-start | bytes 294920 | tf_op jit(solution)/shard_map/ppermute | solution.py:19
  132.2 7.5 %collective-permute-start.8 = (bf16[12,32,128]{2,1,0:T(8,128)(2,1)}, bf16[12,32,128]{2,1,0:T(8,128)(2,1)S(1)}, u32[]{:S(2)}, u32[]{:S(2)}) collective-permute-start(bf16[12,32,128]{2,1,0:T(8,128)(2,1)} %get-tuple-element.211), channel_id=1, source_target_pairs={{0,1},{1,2},{2,3},{3,4},{4,5},{5,6},{6,7},{7,0},{8,9},{9,10},{10,1... | collective-permute-start | bytes 294920 | tf_op jit(solution)/shard_map/ppermute | solution.py:18
  141.1 31.3 %copy-start.3 = (bf16[12,128,128]{2,1,0:T(8,128)(2,1)S(1)}, bf16[12,128,128]{2,1,0:T(8,128)(2,1)}, u32[]{:S(2)}) copy-start(bf16[12,128,128]{2,1,0:T(8,128)(2,1)} %param.29) | copy-start | bytes 1179652
  175.4 7.8 %collective-permute-start.1 = (bf16[12,32,128]{2,0,1:T(8,128)(2,1)S(1)}, bf16[12,32,128]{2,0,1:T(8,128)(2,1)S(1)}, u32[]{:S(2)}, u32[]{:S(2)}) collective-permute-start(bf16[12,32,128]{2,0,1:T(8,128)(2,1)S(1)} %convert_element_type.172), channel_id=1, source_target_pairs={{0,1},{1,2},{2,3},{3,4},{4,5},{5,6},{6,7},{7,0},{8,9},{9,10},{10,1... | collective-permute-start | bytes 294920 | tf_op jit(solution)/shard_map/while/body/eval_jaxpr/ppermute | solution.py:18
  176.9 6.9 %collective-permute-start = (bf16[12,32,128]{2,0,1:T(8,128)(2,1)S(1)}, bf16[12,32,128]{2,0,1:T(8,128)(2,1)}, u32[]{:S(2)}, u32[]{:S(2)}) collective-permute-start(bf16[12,32,128]{2,0,1:T(8,128)(2,1)S(1)} %convert_element_type.172), channel_id=1, source_target_pairs={{1,0},{2,1},{3,2},{4,3},{5,4},{6,5},{7,6},{0,7},{9,8},{10,9},{11,1... | collective-permute-start | bytes 294920 | tf_op jit(solution)/shard_map/while/body/eval_jaxpr/ppermute | solution.py:19
  187.9 7.8 %collective-permute-start.1 = (bf16[12,32,128]{2,0,1:T(8,128)(2,1)S(1)}, bf16[12,32,128]{2,0,1:T(8,128)(2,1)S(1)}, u32[]{:S(2)}, u32[]{:S(2)}) collective-permute-start(bf16[12,32,128]{2,0,1:T(8,128)(2,1)S(1)} %convert_element_type.172), channel_id=1, source_target_pairs={{0,1},{1,2},{2,3},{3,4},{4,5},{5,6},{6,7},{7,0},{8,9},{9,10},{10,1... | collective-permute-start | bytes 294920 | tf_op jit(solution)/shard_map/while/body/eval_jaxpr/ppermute | solution.py:18
  189.4 7.0 %collective-permute-start = (bf16[12,32,128]{2,0,1:T(8,128)(2,1)S(1)}, bf16[12,32,128]{2,0,1:T(8,128)(2,1)}, u32[]{:S(2)}, u32[]{:S(2)}) collective-permute-start(bf16[12,32,128]{2,0,1:T(8,128)(2,1)S(1)} %convert_element_type.172), channel_id=1, source_target_pairs={{1,0},{2,1},{3,2},{4,3},{5,4},{6,5},{7,6},{0,7},{9,8},{10,9},{11,1... | collective-permute-start | bytes 294920 | tf_op jit(solution)/shard_map/while/body/eval_jaxpr/ppermute | solution.py:19
  200.5 7.8 %collective-permute-start.1 = (bf16[12,32,128]{2,0,1:T(8,128)(2,1)S(1)}, bf16[12,32,128]{2,0,1:T(8,128)(2,1)S(1)}, u32[]{:S(2)}, u32[]{:S(2)}) collective-permute-start(bf16[12,32,128]{2,0,1:T(8,128)(2,1)S(1)} %convert_element_type.172), channel_id=1, source_target_pairs={{0,1},{1,2},{2,3},{3,4},{4,5},{5,6},{6,7},{7,0},{8,9},{9,10},{10,1... | collective-permute-start | bytes 294920 | tf_op jit(solution)/shard_map/while/body/eval_jaxpr/ppermute | solution.py:18
  201.9 7.0 %collective-permute-start = (bf16[12,32,128]{2,0,1:T(8,128)(2,1)S(1)}, bf16[12,32,128]{2,0,1:T(8,128)(2,1)}, u32[]{:S(2)}, u32[]{:S(2)}) collective-permute-start(bf16[12,32,128]{2,0,1:T(8,128)(2,1)S(1)} %convert_element_type.172), channel_id=1, source_target_pairs={{1,0},{2,1},{3,2},{4,3},{5,4},{6,5},{7,6},{0,7},{9,8},{10,9},{11,1... | collective-permute-start | bytes 294920 | tf_op jit(solution)/shard_map/while/body/eval_jaxpr/ppermute | solution.py:19
  213.0 7.8 %collective-permute-start.1 = (bf16[12,32,128]{2,0,1:T(8,128)(2,1)S(1)}, bf16[12,32,128]{2,0,1:T(8,128)(2,1)S(1)}, u32[]{:S(2)}, u32[]{:S(2)}) collective-permute-start(bf16[12,32,128]{2,0,1:T(8,128)(2,1)S(1)} %convert_element_type.172), channel_id=1, source_target_pairs={{0,1},{1,2},{2,3},{3,4},{4,5},{5,6},{6,7},{7,0},{8,9},{9,10},{10,1... | collective-permute-start | bytes 294920 | tf_op jit(solution)/shard_map/while/body/eval_jaxpr/ppermute | solution.py:18
  214.4 7.0 %collective-permute-start = (bf16[12,32,128]{2,0,1:T(8,128)(2,1)S(1)}, bf16[12,32,128]{2,0,1:T(8,128)(2,1)}, u32[]{:S(2)}, u32[]{:S(2)}) collective-permute-start(bf16[12,32,128]{2,0,1:T(8,128)(2,1)S(1)} %convert_element_type.172), channel_id=1, source_target_pairs={{1,0},{2,1},{3,2},{4,3},{5,4},{6,5},{7,6},{0,7},{9,8},{10,9},{11,1... | collective-permute-start | bytes 294920 | tf_op jit(solution)/shard_map/while/body/eval_jaxpr/ppermute | solution.py:19
  225.5 7.8 %collective-permute-start.1 = (bf16[12,32,128]{2,0,1:T(8,128)(2,1)S(1)}, bf16[12,32,128]{2,0,1:T(8,128)(2,1)S(1)}, u32[]{:S(2)}, u32[]{:S(2)}) collective-permute-start(bf16[12,32,128]{2,0,1:T(8,128)(2,1)S(1)} %convert_element_type.172), channel_id=1, source_target_pairs={{0,1},{1,2},{2,3},{3,4},{4,5},{5,6},{6,7},{7,0},{8,9},{9,10},{10,1... | collective-permute-start | bytes 294920 | tf_op jit(solution)/shard_map/while/body/eval_jaxpr/ppermute | solution.py:18
  227.0 7.0 %collective-permute-start = (bf16[12,32,128]{2,0,1:T(8,128)(2,1)S(1)}, bf16[12,32,128]{2,0,1:T(8,128)(2,1)}, u32[]{:S(2)}, u32[]{:S(2)}) collective-permute-start(bf16[12,32,128]{2,0,1:T(8,128)(2,1)S(1)} %convert_element_type.172), channel_id=1, source_target_pairs={{1,0},{2,1},{3,2},{4,3},{5,4},{6,5},{7,6},{0,7},{9,8},{10,9},{11,1... | collective-permute-start | bytes 294920 | tf_op jit(solution)/shard_map/while/body/eval_jaxpr/ppermute | solution.py:19
  238.1 7.8 %collective-permute-start.1 = (bf16[12,32,128]{2,0,1:T(8,128)(2,1)S(1)}, bf16[12,32,128]{2,0,1:T(8,128)(2,1)S(1)}, u32[]{:S(2)}, u32[]{:S(2)}) collective-permute-start(bf16[12,32,128]{2,0,1:T(8,128)(2,1)S(1)} %convert_element_type.172), channel_id=1, source_target_pairs={{0,1},{1,2},{2,3},{3,4},{4,5},{5,6},{6,7},{7,0},{8,9},{9,10},{10,1... | collective-permute-start | bytes 294920 | tf_op jit(solution)/shard_map/while/body/eval_jaxpr/ppermute | solution.py:18
  239.5 7.0 %collective-permute-start = (bf16[12,32,128]{2,0,1:T(8,128)(2,1)S(1)}, bf16[12,32,128]{2,0,1:T(8,128)(2,1)}, u32[]{:S(2)}, u32[]{:S(2)}) collective-permute-start(bf16[12,32,128]{2,0,1:T(8,128)(2,1)S(1)} %convert_element_type.172), channel_id=1, source_target_pairs={{1,0},{2,1},{3,2},{4,3},{5,4},{6,5},{7,6},{0,7},{9,8},{10,9},{11,1... | collective-permute-start | bytes 294920 | tf_op jit(solution)/shard_map/while/body/eval_jaxpr/ppermute | solution.py:19
  250.6 7.7 %collective-permute-start.1 = (bf16[12,32,128]{2,0,1:T(8,128)(2,1)S(1)}, bf16[12,32,128]{2,0,1:T(8,128)(2,1)S(1)}, u32[]{:S(2)}, u32[]{:S(2)}) collective-permute-start(bf16[12,32,128]{2,0,1:T(8,128)(2,1)S(1)} %convert_element_type.172), channel_id=1, source_target_pairs={{0,1},{1,2},{2,3},{3,4},{4,5},{5,6},{6,7},{7,0},{8,9},{9,10},{10,1... | collective-permute-start | bytes 294920 | tf_op jit(solution)/shard_map/while/body/eval_jaxpr/ppermute | solution.py:18
  251.1 7.9 %collective-permute-start = (bf16[12,32,128]{2,0,1:T(8,128)(2,1)S(1)}, bf16[12,32,128]{2,0,1:T(8,128)(2,1)}, u32[]{:S(2)}, u32[]{:S(2)}) collective-permute-start(bf16[12,32,128]{2,0,1:T(8,128)(2,1)S(1)} %convert_element_type.172), channel_id=1, source_target_pairs={{1,0},{2,1},{3,2},{4,3},{5,4},{6,5},{7,6},{0,7},{9,8},{10,9},{11,1... | collective-permute-start | bytes 294920 | tf_op jit(solution)/shard_map/while/body/eval_jaxpr/ppermute | solution.py:19
  265.8 6.4 %collective-permute-start.11 = (bf16[12,32,128]{2,1,0:T(8,128)(2,1)S(1)}, bf16[12,32,128]{2,1,0:T(8,128)(2,1)S(1)}, u32[]{:S(2)}, u32[]{:S(2)}) collective-permute-start(bf16[12,32,128]{2,1,0:T(8,128)(2,1)S(1)} %get-tuple-element.213), channel_id=1, source_target_pairs={{1,0},{2,1},{3,2},{4,3},{5,4},{6,5},{7,6},{0,7},{9,8},{10,9},{11,1... | collective-permute-start | bytes 294920 | tf_op jit(solution)/shard_map/ppermute | solution.py:19
  270.0 7.3 %collective-permute-start.10 = (bf16[12,32,128]{2,1,0:T(8,128)(2,1)S(1)}, bf16[12,32,128]{2,1,0:T(8,128)(2,1)S(1)}, u32[]{:S(2)}, u32[]{:S(2)}) collective-permute-start(bf16[12,32,128]{2,1,0:T(8,128)(2,1)S(1)} %get-tuple-element.213), channel_id=1, source_target_pairs={{0,1},{1,2},{2,3},{3,4},{4,5},{5,6},{6,7},{7,0},{8,9},{9,10},{10,1... | collective-permute-start | bytes 294920 | tf_op jit(solution)/shard_map/ppermute | solution.py:18
  303.9 12.0 %collective-permute-start.13 = (bf16[48,32,128]{2,1,0:T(8,128)(2,1)S(1)}, bf16[48,32,128]{2,1,0:T(8,128)(2,1)S(1)}, u32[]{:S(2)}, u32[]{:S(2)}) collective-permute-start(bf16[48,32,128]{2,1,0:T(8,128)(2,1)S(1)} %get-tuple-element.215), channel_id=1, source_target_pairs={{1,0},{2,1},{3,2},{4,3},{5,4},{6,5},{7,6},{0,7},{9,8},{10,9},{11,1... | collective-permute-start | bytes 1179656 | tf_op jit(solution)/shard_map/ppermute | solution.py:19
  305.1 10.8 %collective-permute-start.12 = (bf16[48,32,128]{2,1,0:T(8,128)(2,1)S(1)}, bf16[48,32,128]{2,1,0:T(8,128)(2,1)S(1)}, u32[]{:S(2)}, u32[]{:S(2)}) collective-permute-start(bf16[48,32,128]{2,1,0:T(8,128)(2,1)S(1)} %get-tuple-element.215), channel_id=1, source_target_pairs={{0,1},{1,2},{2,3},{3,4},{4,5},{5,6},{6,7},{7,0},{8,9},{9,10},{10,1... | collective-permute-start | bytes 1179656 | tf_op jit(solution)/shard_map/ppermute | solution.py:18
  (24 other events, 148.7 us)
Sparse Core Ops, SparseCore 0:
  143.7 28.6 all-reduce.1
where the time goes:
time: 339 us; the launch traced here: 334 us
  waiting for transfers between devices  137 us (40%)
  matrix products  82.9 us (24%)
  starting transfers between devices  65.3 us (19%)
  blocking collectives  17.1 us (5%)
  between operations  14.4 us (4%)
  local copies, waits for them, and re-layouts  11.9 us (4%)
  other arithmetic  4.46 us (1%)
    dot_general x14, matrix products, smooth_tiles(): jnp.einsum('iuw,irw->iru', smoother, resid.astype(jnp.bfloat16), preferre...  44.7 us
    ppermute x13, starting transfers between devices, extended(): after = lax.ppermute(first, axis, down)  42.9 us
    ppermute x13, waiting for transfers between devices, extended(): after = lax.ppermute(first, axis, down)  39.6 us
    all_to_all x1, waiting for transfers between devices, on_device(): lax.all_to_all(send_rows, 'blk', split_axis=0, concat_axis=0, tiled=True)  35.3 us
    ppermute x13, waiting for transfers between devices, extended(): before = lax.ppermute(last, axis, up)  33.6 us
    psum x1, waiting for transfers between devices, on_device(): lax.psum(low_terms.astype(jnp.bfloat16), 'fold').astype(jnp.float32)  28.8 us
    all_to_all x1, blocking collectives, on_device(): lax.all_to_all(answers.astype(jnp.bfloat16), 'blk', split_axis=0, concat_...  17.1 us
    dot_general x13, matrix products, apply_tiles(): jnp.einsum('ikj,jrw->ikrw', chooser, widened, preferred_element_type=jnp....  15.6 us
  transfers between devices with their start and end apart: 29, of which 20 were waited for; matrix products, arithmetic and copies ran while one was open for 5% of the time, Pallas kernels for 0%

commit v1 on v0

v1 whole, which is shorter than its diff:
```python
import functools

import jax
import jax.numpy as jnp
from jax import lax
from jax.experimental import pallas as pl
from jax.experimental.pallas import tpu as pltpu
from jax.sharding import PartitionSpec as P

COARSE = 8
F32 = jnp.float32
BF16 = jnp.bfloat16
NT = (((1,), (1,)), ((), ()))
VMEM = pl.BlockSpec(memory_space=pltpu.VMEM)
SMEM = pl.BlockSpec(memory_space=pltpu.SMEM)
MIB = 1 << 20


def sds(shape, dtype):
    return jax.ShapeDtypeStruct(shape, dtype)


def params(mib):
    return pltpu.CompilerParams(vmem_limit_bytes=mib * MIB)


def times(x, tile):
    return lax.dot_general(x, tile, NT, preferred_element_type=F32)


def row_product(cols_ref, base, x_ref, tiles_ref, i):
    count = tiles_ref.shape[1]
    picked = [x_ref[cols_ref[base + k]] for k in range(count)]
    x = jnp.concatenate(picked, axis=1).astype(BF16)
    t = jnp.concatenate([tiles_ref[i, k] for k in range(count)], axis=1)
    return times(x, t)


def fill(dest, parts):
    at = 0
    for part in parts:
        dest[at : at + part.shape[0]] = part[...].astype(dest.dtype)
        at += part.shape[0]


def in_groups(count):
    return next(g for g in (8, 6, 4, 3, 2, 1) if count % g == 0)


def ring(axis):
    n = lax.axis_size(axis)
    return [(i, (i + 1) % n) for i in range(n)], [((i + 1) % n, i) for i in range(n)]


def halos(value):
    up, down = ring("blk")
    return lax.ppermute(value, "blk", up), lax.ppermute(value, "blk", down)


def fine_first(smoother, rhs):
    n, r, vb = rhs.shape
    g = in_groups(n)

    def kernel(m_ref, rhs_ref, f_ref, h_ref):
        for i in range(g):
            v = times(rhs_ref[i].astype(BF16), m_ref[i])
            f_ref[i] = v
            h_ref[i] = v.astype(BF16)

    field = pl.BlockSpec((g, r, vb), lambda s: (s, 0, 0))
    return pl.pallas_call(
        kernel,
        grid=(n // g,),
        in_specs=[pl.BlockSpec((g, vb, vb), lambda s: (s, 0, 0)), field],
        out_specs=[field, field],
        out_shape=[sds(rhs.shape, F32), sds(rhs.shape, BF16)],
        compiler_params=params(24),
    )(smoother, rhs)


def fine_sweep(cols, x3, tiles, smoother, rhs, field):
    n, r, vb = rhs.shape
    kt = tiles.shape[1]
    g = in_groups(n)

    def kernel(cols_ref, a_ref, b_ref, c_ref, t_ref, m_ref, rhs_ref, v_ref, f_ref, h_ref, x_ref):
        s = pl.program_id(0)

        @pl.when(s == 0)
        def _():
            fill(x_ref, (a_ref, b_ref, c_ref))

        for i in range(g):
            z = rhs_ref[i] - row_product(cols_ref, (s * g + i) * kt, x_ref, t_ref, i)
            v = v_ref[i] + times(z.astype(BF16), m_ref[i])
            f_ref[i] = v
            h_ref[i] = v.astype(BF16)

    whole = pl.BlockSpec((n, r, vb), lambda s, c: (0, 0, 0))
    block = pl.BlockSpec((g, r, vb), lambda s, c: (s, 0, 0))
    return pl.pallas_call(
        kernel,
        grid_spec=pltpu.PrefetchScalarGridSpec(
            num_scalar_prefetch=1,
            grid=(n // g,),
            in_specs=[whole] * 3
            + [
                pl.BlockSpec((g, kt, vb, vb), lambda s, c: (s, 0, 0, 0)),
                pl.BlockSpec((g, vb, vb), lambda s, c: (s, 0, 0)),
                block,
                block,
            ],
            out_specs=[block, block],
            scratch_shapes=[pltpu.VMEM((3 * n, r, vb), BF16)],
        ),
        out_shape=[sds(rhs.shape, F32), sds(rhs.shape, BF16)],
        compiler_params=params(32),
    )(cols, *x3, tiles, smoother, rhs, field)


def one_hot(slots_row, vb):
    return (lax.broadcasted_iota(jnp.int32, (vb, vb), 0) == slots_row).astype(F32).astype(BF16)


def collected(z, slots_row):
    r, vb = z.shape
    high = z.astype(BF16)
    low = (z - high.astype(F32)).astype(BF16)
    both = times(jnp.concatenate([high, low], axis=0), one_hot(slots_row, vb))
    return both[:r] + both[r:]


def fine_restrict(cols, target, x3, tiles, rhs, slots, mids):
    n, r, vb = rhs.shape
    kt = tiles.shape[1]
    g = in_groups(n)
    steps = n // g

    def kernel(cols_ref, to_ref, a_ref, b_ref, c_ref, t_ref, rhs_ref, s_ref, z_ref, o_ref, x_ref, acc_ref):
        s = pl.program_id(0)

        @pl.when(s == 0)
        def _():
            fill(x_ref, (a_ref, b_ref, c_ref))
            acc_ref[...] = jnp.zeros_like(acc_ref)

        for i in range(g):
            z = rhs_ref[i] - row_product(cols_ref, (s * g + i) * kt, x_ref, t_ref, i)
            z_ref[i] = z
            acc_ref[to_ref[s * g + i]] += collected(z, s_ref[i : i + 1, :])

        @pl.when(s == steps - 1)
        def _():
            o_ref[...] = acc_ref[...].astype(BF16)

    whole = pl.BlockSpec((n, r, vb), lambda s, c, t: (0, 0, 0))
    block = pl.BlockSpec((g, r, vb), lambda s, c, t: (s, 0, 0))
    return pl.pallas_call(
        kernel,
        grid_spec=pltpu.PrefetchScalarGridSpec(
            num_scalar_prefetch=2,
            grid=(steps,),
            in_specs=[whole] * 3
            + [
                pl.BlockSpec((g, kt, vb, vb), lambda s, c, t: (s, 0, 0, 0)),
                block,
                pl.BlockSpec((g, vb), lambda s, c, t: (s, 0)),
            ],
            out_specs=[block, pl.BlockSpec((mids, r, vb), lambda s, c, t: (0, 0, 0))],
            scratch_shapes=[pltpu.VMEM((3 * n, r, vb), BF16), pltpu.VMEM((mids, r, vb), F32)],
        ),
        out_shape=[sds(rhs.shape, F32), sds((mids, r, vb), BF16)],
        compiler_params=params(40),
    )(cols, target, *x3, tiles, rhs, slots)


def fine_last(cols, target3, order, slots3, mid_parts, tiles, smoother, resid, field):
    n, r, vb = resid.shape
    kt = tiles.shape[1]
    g = in_groups(n)
    parts = len(mid_parts)
    per = mid_parts[0].shape[0]

    def kernel(cols_ref, to_ref, order_ref, *refs):
        s_ref, mid_refs, (t_ref, m_ref, z_ref, v_ref, f_ref, x_ref, all_ref) = (
            refs[0],
            refs[1 : 1 + parts],
            refs[1 + parts :],
        )
        s = pl.program_id(0)

        @pl.when(s == 0)
        def _():
            for p in range(parts):
                all_ref[pl.ds(order_ref[p] * per, per)] = mid_refs[p][...].astype(F32)

            def some(j, carry):
                for q in range(g):
                    i = j * g + q
                    index = jnp.broadcast_to(s_ref[pl.ds(i, 1), :], (r, vb))
                    x_ref[i] = jnp.take_along_axis(all_ref[to_ref[i]], index, axis=1).astype(BF16)
                return carry

            lax.fori_loop(0, 3 * n // g, some, 0)

        for i in range(g):
            z = z_ref[i] - row_product(cols_ref, (s * g + i) * kt, x_ref, t_ref, i)
            f_ref[i] = v_ref[i] + x_ref[n + s * g + i].astype(F32) + times(z.astype(BF16), m_ref[i])

    def const(*shape):
        return pl.BlockSpec(shape, lambda s, c, t, o: (0,) * len(shape))

    block = pl.BlockSpec((g, r, vb), lambda s, c, t, o: (s, 0, 0))
    return pl.pallas_call(
        kernel,
        grid_spec=pltpu.PrefetchScalarGridSpec(
            num_scalar_prefetch=3,
            grid=(n // g,),
            in_specs=[const(3 * n, vb)]
            + [const(per, r, vb)] * parts
            + [
                pl.BlockSpec((g, kt, vb, vb), lambda s, c, t, o: (s, 0, 0, 0)),
                pl.BlockSpec((g, vb, vb), lambda s, c, t, o: (s, 0, 0)),
                block,
                block,
            ],
            out_specs=[block],
            scratch_shapes=[pltpu.VMEM((3 * n, r, vb), BF16), pltpu.VMEM((parts * per, r, vb), F32)],
        ),
        out_shape=[sds(resid.shape, F32)],
        compiler_params=params(40),
    )(cols, target3, order, slots3, *mid_parts, tiles, smoother, resid, field)[0]


def add_and_smooth(smoother, terms):
    shape = terms[0].shape

    def kernel(m_ref, *refs):
        term_refs, (rhs_ref, f_ref, h_ref) = refs[:-3], refs[-3:]
        for i in range(shape[0]):
            total = term_refs[0][i].astype(F32)
            for t in term_refs[1:]:
                total = total + t[i].astype(F32)
            rhs_ref[i] = total
            v = times(total.astype(BF16), m_ref[i])
            f_ref[i] = v
            h_ref[i] = v.astype(BF16)

    return pl.pallas_call(
        kernel,
        in_specs=[VMEM] * (1 + len(terms)),
        out_specs=[VMEM] * 3,
        out_shape=[sds(shape, F32), sds(shape, F32), sds(shape, BF16)],
        compiler_params=params(16),
    )(smoother, *terms)


def small_sweep(cols, x3, tiles, smoother, rhs, field):
    n, r, vb = rhs.shape
    kt = tiles.shape[1]
    pick = BF16 if r % 16 == 0 else F32

    def kernel(cols_ref, a_ref, b_ref, c_ref, t_ref, m_ref, rhs_ref, v_ref, f_ref, h_ref, x_ref):
        fill(x_ref, (a_ref, b_ref, c_ref))
        for i in range(n):
            z = rhs_ref[i] - row_product(cols_ref, i * kt, x_ref, t_ref, i)
            v = v_ref[i] + times(z.astype(BF16), m_ref[i])
            f_ref[i] = v
            h_ref[i] = v.astype(BF16)

    return pl.pallas_call(
        kernel,
        in_specs=[SMEM] + [VMEM] * 7,
        out_specs=[VMEM] * 2,
        out_shape=[sds(rhs.shape, F32), sds(rhs.shape, BF16)],
        scratch_shapes=[pltpu.VMEM((3 * n, r, vb), pick)],
        compiler_params=params(24),
    )(cols, *x3, tiles, smoother, rhs, field)


def mid_restrict(cols, target, order, x3, tiles, rhs, slots, lows, folds):
    n, r, vb = rhs.shape
    kt = tiles.shape[1]
    share = r // folds

    def kernel(cols_ref, to_ref, order_ref, a_ref, b_ref, c_ref, t_ref, rhs_ref, s_ref, *refs):
        outs, (x_ref, acc_ref, cut_ref) = refs[:folds], refs[folds:]
        fill(x_ref, (a_ref, b_ref, c_ref))
        acc_ref[...] = jnp.zeros_like(acc_ref)
        for i in range(n):
            z = rhs_ref[i] - row_product(cols_ref, i * kt, x_ref, t_ref, i)
            acc_ref[to_ref[i]] += collected(z, s_ref[i : i + 1, :])
        for f in range(folds):
            cut_ref[f] = acc_ref[:, f * share : (f + 1) * share, :]
        for f in range(folds):
            outs[f][...] = cut_ref[order_ref[f]].astype(BF16)

    return pl.pallas_call(
        kernel,
        in_specs=[SMEM] * 3 + [VMEM] * 6,
        out_specs=[VMEM] * folds,
        out_shape=[sds((lows, share, vb), BF16)] * folds,
        scratch_shapes=[
            pltpu.VMEM((3 * n, r, vb), BF16),
            pltpu.VMEM((lows, r, vb), F32),
            pltpu.VMEM((folds, lows, share, vb), F32),
        ],
        compiler_params=params(24),
    )(cols, target, order, *x3, tiles, rhs, slots)


def mid_lift(target, order, parts, field, slots):
    n, r, vb = field.shape
    folds = len(parts)
    lows, share = parts[0].shape[:2]

    def kernel(to_ref, order_ref, *refs):
        part_refs, (v_ref, s_ref, c_ref, f_ref, h_ref, cut_ref) = refs[:folds], refs[folds:]
        for f in range(folds):
            cut_ref[order_ref[f]] = part_refs[f][...].astype(F32)
        for f in range(folds):
            c_ref[:, f * share : (f + 1) * share, :] = cut_ref[f]
        for i in range(n):
            index = jnp.broadcast_to(s_ref[i : i + 1, :], (r, vb))
            v = v_ref[i] + jnp.take_along_axis(c_ref[to_ref[i]], index, axis=1)
            f_ref[i] = v
            h_ref[i] = v.astype(BF16)

    return pl.pallas_call(
        kernel,
        in_specs=[SMEM] * 2 + [VMEM] * (folds + 2),
        out_specs=[VMEM] * 3,
        out_shape=[sds((lows, r, vb), F32), sds(field.shape, F32), sds(field.shape, BF16)],
        scratch_shapes=[pltpu.VMEM((folds, lows, share, vb), F32)],
        compiler_params=params(16),
    )(target, order, *parts, field, slots)


def local_columns(columns, per_device):
    blks = lax.axis_size("blk")
    owner = columns // per_device % blks
    offset = (owner - lax.axis_index("blk") + 1 + blks) % blks
    return (offset * per_device + columns % per_device).reshape(-1)


def on_device(
    fine_rhs,
    fine_tiles,
    fine_cols,
    fine_smoother,
    fine_map,
    fine_slots,
    mid_tiles,
    mid_cols,
    mid_smoother,
    mid_map,
    mid_slots,
    coarse_tiles,
    coarse_cols,
    coarse_smoother,
):
    n0, r, vb = fine_rhs.shape
    n1 = mid_tiles.shape[0]
    n2 = coarse_tiles.shape[0]
    blks, folds = lax.axis_size("blk"), lax.axis_size("fold")
    blk, fold = lax.axis_index("blk"), lax.axis_index("fold")
    cols0 = local_columns(fine_cols, n0)
    cols1 = local_columns(mid_cols, n1)
    cols2 = local_columns(coarse_cols, n2)
    to_mid = fine_map % (blks * n1)
    to_low = mid_map % n2

    v, h = fine_first(fine_smoother, fine_rhs)
    before, after = halos(h)
    map_rows = -(-n0 // vb)
    table = jnp.concatenate(
        [fine_slots, jnp.pad(to_mid, (0, map_rows * vb - n0)).reshape(map_rows, vb)], axis=0
    )
    table_before, table_after = halos(table)
    v, h = fine_sweep(cols0, (before, h, after), fine_tiles, fine_smoother, fine_rhs, v)
    before, after = halos(h)
    resid, sums = fine_restrict(
        cols0, to_mid, (before, h, after), fine_tiles, fine_rhs, fine_slots, blks * n1
    )
    received = lax.all_to_all(
        sums.reshape(blks, n1, r, vb), "blk", split_axis=0, concat_axis=0, tiled=True
    )

    mid_rhs, w, h = add_and_smooth(mid_smoother, [received[k] for k in range(blks)])
    before, after = halos(h)
    w, h = small_sweep(cols1, (before, h, after), mid_tiles, mid_smoother, mid_rhs, w)
    before, after = halos(h)
    there = (fold + jnp.arange(folds, dtype=jnp.int32)) % folds
    back = (fold - jnp.arange(folds, dtype=jnp.int32)) % folds
    cuts = mid_restrict(
        cols1, to_low, there, (before, h, after), mid_tiles, mid_rhs, mid_slots, n2, folds
    )

    shifts = [[(i, (i + k) % folds) for i in range(folds)] for k in range(folds)]
    terms = [cuts[0]] + [lax.ppermute(cuts[k], "fold", shifts[k]) for k in range(1, folds)]
    low_rhs, c, h = add_and_smooth(coarse_smoother, terms)
    for _ in range(COARSE - 1):
        before, after = halos(h)
        c, h = small_sweep(cols2, (before, h, after), coarse_tiles, coarse_smoother, low_rhs, c)
    parts = [h] + [lax.ppermute(h, "fold", shifts[k]) for k in range(1, folds)]

    coarse_field, w, h = mid_lift(to_low, back, parts, w, mid_slots)
    before, after = halos(h)
    mid_field, h = small_sweep(cols1, (before, h, after), mid_tiles, mid_smoother, mid_rhs, w)

    mids = [h] + [
        lax.ppermute(h, "blk", [(i, (i + k) % blks) for i in range(blks)]) for k in range(1, blks)
    ]
    order = (blk - jnp.arange(blks, dtype=jnp.int32)) % blks
    slots3 = jnp.concatenate([table_before[:n0], fine_slots, table_after[:n0]], axis=0)
    target3 = jnp.concatenate(
        [table_before[n0:].reshape(-1)[:n0], to_mid, table_after[n0:].reshape(-1)[:n0]]
    )
    fine_field = fine_last(
        cols0, target3, order, slots3, mids, fine_tiles, fine_smoother, resid, v
    )
    return fine_field, mid_field, coarse_field


def solution(mesh):
    both = ("fold", "blk")
    return jax.shard_map(
        on_device,
        mesh=mesh,
        in_specs=(
            P(both, None, None),
            P(both, None, None, None),
            P(both, None),
            P(both, None, None),
            P(both),
            P(both, None),
            P(both, None, None, None),
            P(both, None),
            P(both, None, None),
            P(both),
            P(both, None),
            P("blk", None, None, None),
            P("blk", None),
            P("blk", None, None),
        ),
        out_specs=(P(both, None, None), P(both, None, None), P("blk", None, None)),
        check_vma=False,
    )
```

time: 339 us -> 241 us (0.71)
  matrix products: 82.9 us -> 0 us
  Pallas kernels: 0 us -> 66.6 us
  waiting for transfers between devices: 137 us -> 77.4 us
  blocking collectives: 17.1 us -> 0 us
  starting transfers between devices: 65.3 us -> 82 us
  between operations: 14.4 us -> 0.92 us
  other arithmetic: 4.46 us -> 0.21 us
    dot_general x39 -> x0, matrix products: 82.9 us -> none  [the longest x14 44.7 us: smooth_tiles(): jnp.einsum('iuw,irw->iru', smoother, resid.astype(jnp.bfloat16), preferre...]
    pallas_call x0 -> x17, Pallas kernels: none -> 66.6 us  [the longest x9 28.9 us: small_sweep(): pl.pallas_call(kernel, in_specs=[SMEM] + [VMEM] * 7, out_specs=[VMEM] * 2...]
    psum x1 -> x0, waiting for transfers between devices: 28.8 us -> none  [on_device(): lax.psum(low_terms.astype(jnp.bfloat16), 'fold').astype(jnp.float32)]
    ppermute x26 -> x39, starting transfers between devices: 54.9 us -> 77.6 us  [the longest x26 60.6 us: halos(): return (lax.ppermute(value, 'blk', up), lax.ppermute(value, 'blk', down))]
    all_to_all x1 -> x0, blocking collectives: 17.1 us -> none  [on_device(): lax.all_to_all(answers.astype(jnp.bfloat16), 'blk', split_axis=0, concat_...]
    ppermute x26 -> x39, waiting for transfers between devices: 73.2 us -> 57.1 us  [the longest x26 48.8 us: halos(): return (lax.ppermute(value, 'blk', up), lax.ppermute(value, 'blk', down))]
    all_to_all x2 -> x1, waiting for transfers between devices: 35.4 us -> 20.3 us  [on_device(): lax.all_to_all(sums.reshape(blks, n1, r, vb), 'blk', split_axis=0, concat...]
    while x16 -> x0, local copies, waits for them, and re-layouts: 6.25 us -> none
  transfers between devices with their start and end apart: 29 -> 40, of which waited for: 20 -> 21; matrix products, arithmetic and copies ran while one was open for 5% -> 1% of each run, Pallas kernels for 0% -> 5%
where the time goes in v1:
time: 241 us; the launch traced here: 237 us
  starting transfers between devices  82 us (34%)
  waiting for transfers between devices  77.4 us (32%)
  Pallas kernels  66.6 us (28%)
  local copies, waits for them, and re-layouts  9.92 us (4%)
    ppermute x26, starting transfers between devices, halos(): return (lax.ppermute(value, 'blk', up), lax.ppermute(value, 'blk', down))  60.6 us
    ppermute x26, waiting for transfers between devices, halos(): return (lax.ppermute(value, 'blk', up), lax.ppermute(value, 'blk', down))  48.8 us
    pallas_call x9, Pallas kernels, small_sweep(): pl.pallas_call(kernel, in_specs=[SMEM] + [VMEM] * 7, out_specs=[VMEM] * 2...  28.9 us
    all_to_all x1, waiting for transfers between devices, on_device(): lax.all_to_all(sums.reshape(blks, n1, r, vb), 'blk', split_axis=0, concat...  20.3 us
    ppermute x7, starting transfers between devices, on_device(): lax.ppermute(h, 'blk', [(i, (i + k) % blks) for i in range(blks)])  11.8 us
    pallas_call x1, Pallas kernels, fine_last(): pl.pallas_call(kernel, grid_spec=pltpu.PrefetchScalarGridSpec(num_scalar_...  11.6 us
    pallas_call x1, Pallas kernels, fine_sweep(): pl.pallas_call(kernel, grid_spec=pltpu.PrefetchScalarGridSpec(num_scalar_...  10.2 us
    pallas_call x1, Pallas kernels, fine_restrict(): pl.pallas_call(kernel, grid_spec=pltpu.PrefetchScalarGridSpec(num_scalar_...  9.97 us
  transfers between devices with their start and end apart: 40, of which 21 were waited for; matrix products, arithmetic and copies ran while one was open for 1% of the time, Pallas kernels for 5%

profile of v1, /device:TPU:0, one launch (start us, length us, event | category | flops | bytes accessed | tf_op | source)
XLA Modules:
  0.0 237.1 jit_solution(12438804810117810332)
XLA Ops:
  12.4 12.1 %collective-permute-done.2.a_ref = bf16[48,32,128]{2,1,0:T(8,128)(2,1)} collective-permute-done((bf16[48,32,128]{2,1,0:T(8,128)(2,1)S(1)}, bf16[48,32,128]{2,1,0:T(8,128)(2,1)}, u32[]{:S(2)}, u32[]{:S(2)}) %collective-permute-start.2) | collective-permute-done | bytes 393248 | tf_op jit(solution)/shard_map/ppermute | solution.py:57
  26.8 3.2 %copy-done.1 = bf16[48,5,128,128]{3,2,1,0:T(8,128)(2,1)S(1)} copy-done((bf16[48,5,128,128]{3,2,1,0:T(8,128)(2,1)S(1)}, bf16[48,5,128,128]{3,2,1,0:T(8,128)(2,1)}, u32[]{:S(2)}) %copy-start.1) | copy-done | bytes 7864344
  30.0 10.2 %shard_map.158 = (f32[48,32,128]{2,1,0:T(8,128)S(1)}, bf16[48,32,128]{2,1,0:T(8,128)(2,1)S(1)}) custom-call(s32[240]{0:T(256)S(1)} %reshape.25.cols_ref, bf16[48,32,128]{2,1,0:T(8,128)(2,1)} %collective-permute-done.2.a_ref, bf16[48,32,128]{2,1,0:T(8,128)(2,1)S(1)} %get-tuple-element.39.b_ref, bf16[48,32,128]{2,1,0:T(8,128)(2,1)} %collective-permute-done.3.c_ref, ...), custom_call_target="tpu_custom_call" | custom-call | tf_op jit(solution)/shard_map/pallas_call | solution.py:101
  40.6 4.4 %collective-permute-start.5 = (bf16[48,32,128]{2,1,0:T(8,128)(2,1)S(1)}, bf16[48,32,128]{2,1,0:T(8,128)(2,1)S(1)}, u32[]{:S(2)}, u32[]{:S(2)}) collective-permute-start(bf16[48,32,128]{2,1,0:T(8,128)(2,1)S(1)} %get-tuple-element.41.b_ref), channel_id=1, source_target_pairs={{1,0},{2,1},{3,2},{4,3},{5,4},{6,5},{7,6},{0,7},{9,8},{10,9},{11,1... | collective-permute-start | bytes 1179656 | tf_op jit(solution)/shard_map/ppermute | solution.py:57
  45.1 11.5 %collective-permute-done.4.a_ref = bf16[48,32,128]{2,1,0:T(8,128)(2,1)S(1)} collective-permute-done((bf16[48,32,128]{2,1,0:T(8,128)(2,1)S(1)}, bf16[48,32,128]{2,1,0:T(8,128)(2,1)S(1)}, u32[]{:S(2)}, u32[]{:S(2)}) %collective-permute-start.4) | collective-permute-done | bytes 393248 | tf_op jit(solution)/shard_map/ppermute | solution.py:57
  56.5 3.9 %collective-permute-done.5.c_ref = bf16[48,32,128]{2,1,0:T(8,128)(2,1)S(1)} collective-permute-done((bf16[48,32,128]{2,1,0:T(8,128)(2,1)S(1)}, bf16[48,32,128]{2,1,0:T(8,128)(2,1)S(1)}, u32[]{:S(2)}, u32[]{:S(2)}) %collective-permute-start.5) | collective-permute-done | bytes 393248 | tf_op jit(solution)/shard_map/ppermute | solution.py:57
  60.4 10.0 %shard_map.159 = (f32[48,32,128]{2,1,0:T(8,128)S(1)}, bf16[96,32,128]{2,1,0:T(8,128)(2,1)}) custom-call(s32[240]{0:T(256)S(1)} %reshape.25.cols_ref, s32[48]{0:T(128)S(1)} %and_select_fusion.4.to_ref, bf16[48,32,128]{2,1,0:T(8,128)(2,1)S(1)} %collective-permute-done.4.a_ref, bf16[48,32,128]{2,1,0:T(8,128)(2,1)S(1)} %get-tuple-element.41.b_ref, ...), custom_call_target="tpu_custom_call" | custom-call | tf_op jit(solution)/shard_map/pallas_call | solution.py:158
  71.3 4.3 %all-to-all-start = ((bf16[8,12,32,128]{3,2,1,0:T(8,128)(2,1)}), bf16[8,12,32,128]{3,2,1,0:T(8,128)(2,1)}, u32[]{:S(2)}, u32[]{:S(2)}) async-start(bf16[8,12,32,128]{3,2,1,0:T(8,128)(2,1)} %bitcast.3), calls=%async_computation | async-start | bytes 1572864 | tf_op jit(solution)/shard_map/all_to_all | solution.py:385
  75.7 20.3 %all-to-all-done = bf16[8,12,32,128]{3,2,1,0:T(8,128)(2,1)} async-done(((bf16[8,12,32,128]{3,2,1,0:T(8,128)(2,1)}), bf16[8,12,32,128]{3,2,1,0:T(8,128)(2,1)}, u32[]{:S(2)}, u32[]{:S(2)}) %all-to-all-start) | async-done | bytes 786464 | tf_op jit(solution)/shard_map/all_to_all | solution.py:385
  98.7 3.7 %collective-permute-start.7 = (bf16[12,32,128]{2,1,0:T(8,128)(2,1)S(1)}, bf16[12,32,128]{2,1,0:T(8,128)(2,1)S(1)}, u32[]{:S(2)}, u32[]{:S(2)}) collective-permute-start(bf16[12,32,128]{2,1,0:T(8,128)(2,1)S(1)} %get-tuple-element.43.b_ref), channel_id=1, source_target_pairs={{1,0},{2,1},{3,2},{4,3},{5,4},{6,5},{7,6},{0,7},{9,8},{10,9},{11,1... | collective-permute-start | bytes 294920 | tf_op jit(solution)/shard_map/ppermute | solution.py:57
  107.6 4.8 %collective-permute-start.9 = (bf16[12,32,128]{2,1,0:T(8,128)(2,1)S(1)}, bf16[12,32,128]{2,1,0:T(8,128)(2,1)S(1)}, u32[]{:S(2)}, u32[]{:S(2)}) collective-permute-start(bf16[12,32,128]{2,1,0:T(8,128)(2,1)S(1)} %get-tuple-element.46.b_ref), channel_id=1, source_target_pairs={{1,0},{2,1},{3,2},{4,3},{5,4},{6,5},{7,6},{0,7},{9,8},{10,9},{11,1... | collective-permute-start | bytes 294920 | tf_op jit(solution)/shard_map/ppermute | solution.py:57
  122.3 4.8 %collective-permute-start.14 = (bf16[12,8,128]{2,1,0:T(8,128)(2,1)S(1)}, bf16[12,8,128]{2,1,0:T(8,128)(2,1)S(1)}, u32[]{:S(2)}, u32[]{:S(2)}) collective-permute-start(bf16[12,8,128]{2,1,0:T(8,128)(2,1)S(1)} %get-tuple-element.51.b_ref), channel_id=1, source_target_pairs={{1,0},{2,1},{3,2},{4,3},{5,4},{6,5},{7,6},{0,7},{9,8},{10,9},{11,1... | collective-permute-start | bytes 73736 | tf_op jit(solution)/shard_map/ppermute | solution.py:57
  129.1 3.2 %shard_map.164 = (f32[12,8,128]{2,1,0:T(8,128)S(1)}, bf16[12,8,128]{2,1,0:T(8,128)(2,1)S(1)}) custom-call(s32[60]{0:T(128)S(1)} %reshape.28.cols_ref, bf16[12,8,128]{2,1,0:T(8,128)(2,1)S(1)} %collective-permute-done.13.a_ref, bf16[12,8,128]{2,1,0:T(8,128)(2,1)S(1)} %get-tuple-element.51.b_ref, bf16[12,8,128]{2,1,0:T(8,128)(2,1)S(1)} %collective-permute-done.14.c_ref, ...), custom_call_target="tpu_custom_call" | custom-call | tf_op jit(solution)/shard_map/pallas_call | solution.py:271
  132.3 4.8 %collective-permute-start.16 = (bf16[12,8,128]{2,1,0:T(8,128)(2,1)S(1)}, bf16[12,8,128]{2,1,0:T(8,128)(2,1)S(1)}, u32[]{:S(2)}, u32[]{:S(2)}) collective-permute-start(bf16[12,8,128]{2,1,0:T(8,128)(2,1)S(1)} %get-tuple-element.54.b_ref), channel_id=1, source_target_pairs={{1,0},{2,1},{3,2},{4,3},{5,4},{6,5},{7,6},{0,7},{9,8},{10,9},{11,1... | collective-permute-start | bytes 73736 | tf_op jit(solution)/shard_map/ppermute | solution.py:57
  138.9 3.2 %shard_map.165 = (f32[12,8,128]{2,1,0:T(8,128)S(1)}, bf16[12,8,128]{2,1,0:T(8,128)(2,1)S(1)}) custom-call(s32[60]{0:T(128)S(1)} %reshape.28.cols_ref, bf16[12,8,128]{2,1,0:T(8,128)(2,1)S(1)} %collective-permute-done.15.a_ref, bf16[12,8,128]{2,1,0:T(8,128)(2,1)S(1)} %get-tuple-element.54.b_ref, bf16[12,8,128]{2,1,0:T(8,128)(2,1)S(1)} %collective-permute-done.16.c_ref, ...), custom_call_target="tpu_custom_call" | custom-call | tf_op jit(solution)/shard_map/pallas_call | solution.py:271
  142.1 4.8 %collective-permute-start.18 = (bf16[12,8,128]{2,1,0:T(8,128)(2,1)S(1)}, bf16[12,8,128]{2,1,0:T(8,128)(2,1)S(1)}, u32[]{:S(2)}, u32[]{:S(2)}) collective-permute-start(bf16[12,8,128]{2,1,0:T(8,128)(2,1)S(1)} %get-tuple-element.56.b_ref), channel_id=1, source_target_pairs={{1,0},{2,1},{3,2},{4,3},{5,4},{6,5},{7,6},{0,7},{9,8},{10,9},{11,1... | collective-permute-start | bytes 73736 | tf_op jit(solution)/shard_map/ppermute | solution.py:57
  148.7 3.2 %shard_map.166 = (f32[12,8,128]{2,1,0:T(8,128)S(1)}, bf16[12,8,128]{2,1,0:T(8,128)(2,1)S(1)}) custom-call(s32[60]{0:T(128)S(1)} %reshape.28.cols_ref, bf16[12,8,128]{2,1,0:T(8,128)(2,1)S(1)} %collective-permute-done.17.a_ref, bf16[12,8,128]{2,1,0:T(8,128)(2,1)S(1)} %get-tuple-element.56.b_ref, bf16[12,8,128]{2,1,0:T(8,128)(2,1)S(1)} %collective-permute-done.18.c_ref, ...), custom_call_target="tpu_custom_call" | custom-call | tf_op jit(solution)/shard_map/pallas_call | solution.py:271
  151.9 4.8 %collective-permute-start.20 = (bf16[12,8,128]{2,1,0:T(8,128)(2,1)S(1)}, bf16[12,8,128]{2,1,0:T(8,128)(2,1)S(1)}, u32[]{:S(2)}, u32[]{:S(2)}) collective-permute-start(bf16[12,8,128]{2,1,0:T(8,128)(2,1)S(1)} %get-tuple-element.58.b_ref), channel_id=1, source_target_pairs={{1,0},{2,1},{3,2},{4,3},{5,4},{6,5},{7,6},{0,7},{9,8},{10,9},{11,1... | collective-permute-start | bytes 73736 | tf_op jit(solution)/shard_map/ppermute | solution.py:57
  158.5 3.2 %shard_map.167 = (f32[12,8,128]{2,1,0:T(8,128)S(1)}, bf16[12,8,128]{2,1,0:T(8,128)(2,1)S(1)}) custom-call(s32[60]{0:T(128)S(1)} %reshape.28.cols_ref, bf16[12,8,128]{2,1,0:T(8,128)(2,1)S(1)} %collective-permute-done.19.a_ref, bf16[12,8,128]{2,1,0:T(8,128)(2,1)S(1)} %get-tuple-element.58.b_ref, bf16[12,8,128]{2,1,0:T(8,128)(2,1)S(1)} %collective-permute-done.20.c_ref, ...), custom_call_target="tpu_custom_call" | custom-call | tf_op jit(solution)/shard_map/pallas_call | solution.py:271
  161.7 4.8 %collective-permute-start.22 = (bf16[12,8,128]{2,1,0:T(8,128)(2,1)S(1)}, bf16[12,8,128]{2,1,0:T(8,128)(2,1)S(1)}, u32[]{:S(2)}, u32[]{:S(2)}) collective-permute-start(bf16[12,8,128]{2,1,0:T(8,128)(2,1)S(1)} %get-tuple-element.60.b_ref), channel_id=1, source_target_pairs={{1,0},{2,1},{3,2},{4,3},{5,4},{6,5},{7,6},{0,7},{9,8},{10,9},{11,1... | collective-permute-start | bytes 73736 | tf_op jit(solution)/shard_map/ppermute | solution.py:57
  168.6 3.2 %shard_map.168 = (f32[12,8,128]{2,1,0:T(8,128)S(1)}, bf16[12,8,128]{2,1,0:T(8,128)(2,1)S(1)}) custom-call(s32[60]{0:T(128)S(1)} %reshape.28.cols_ref, bf16[12,8,128]{2,1,0:T(8,128)(2,1)S(1)} %collective-permute-done.21.a_ref, bf16[12,8,128]{2,1,0:T(8,128)(2,1)S(1)} %get-tuple-element.60.b_ref, bf16[12,8,128]{2,1,0:T(8,128)(2,1)S(1)} %collective-permute-done.22.c_ref, ...), custom_call_target="tpu_custom_call" | custom-call | tf_op jit(solution)/shard_map/pallas_call | solution.py:271
  171.8 4.7 %collective-permute-start.24 = (bf16[12,8,128]{2,1,0:T(8,128)(2,1)S(1)}, bf16[12,8,128]{2,1,0:T(8,128)(2,1)S(1)}, u32[]{:S(2)}, u32[]{:S(2)}) collective-permute-start(bf16[12,8,128]{2,1,0:T(8,128)(2,1)S(1)} %get-tuple-element.62.b_ref), channel_id=1, source_target_pairs={{1,0},{2,1},{3,2},{4,3},{5,4},{6,5},{7,6},{0,7},{9,8},{10,9},{11,1... | collective-permute-start | bytes 73736 | tf_op jit(solution)/shard_map/ppermute | solution.py:57
  178.3 3.2 %shard_map.169 = (f32[12,8,128]{2,1,0:T(8,128)S(1)}, bf16[12,8,128]{2,1,0:T(8,128)(2,1)S(1)}) custom-call(s32[60]{0:T(128)S(1)} %reshape.28.cols_ref, bf16[12,8,128]{2,1,0:T(8,128)(2,1)S(1)} %collective-permute-done.23.a_ref, bf16[12,8,128]{2,1,0:T(8,128)(2,1)S(1)} %get-tuple-element.62.b_ref, bf16[12,8,128]{2,1,0:T(8,128)(2,1)S(1)} %collective-permute-done.24.c_ref, ...), custom_call_target="tpu_custom_call" | custom-call | tf_op jit(solution)/shard_map/pallas_call | solution.py:271
  181.6 4.8 %collective-permute-start.26 = (bf16[12,8,128]{2,1,0:T(8,128)(2,1)S(1)}, bf16[12,8,128]{2,1,0:T(8,128)(2,1)S(1)}, u32[]{:S(2)}, u32[]{:S(2)}) collective-permute-start(bf16[12,8,128]{2,1,0:T(8,128)(2,1)S(1)} %get-tuple-element.64.b_ref), channel_id=1, source_target_pairs={{1,0},{2,1},{3,2},{4,3},{5,4},{6,5},{7,6},{0,7},{9,8},{10,9},{11,1... | collective-permute-start | bytes 73736 | tf_op jit(solution)/shard_map/ppermute | solution.py:57
  188.1 3.9 %shard_map.170 = (f32[12,8,128]{2,1,0:T(8,128)}, bf16[12,8,128]{2,1,0:T(8,128)(2,1)S(1)}) custom-call(s32[60]{0:T(128)S(1)} %reshape.28.cols_ref, bf16[12,8,128]{2,1,0:T(8,128)(2,1)S(1)} %collective-permute-done.25.a_ref, bf16[12,8,128]{2,1,0:T(8,128)(2,1)S(1)} %get-tuple-element.64.b_ref, bf16[12,8,128]{2,1,0:T(8,128)(2,1)S(1)} %collective-permute-done.26.c_ref, ...), custom_call_target="tpu_custom_call" | custom-call | tf_op jit(solution)/shard_map/pallas_call | solution.py:271
  197.3 4.7 %collective-permute-start.31 = (bf16[12,32,128]{2,1,0:T(8,128)(2,1)S(1)}, bf16[12,32,128]{2,1,0:T(8,128)(2,1)S(1)}, u32[]{:S(2)}, u32[]{:S(2)}) collective-permute-start(bf16[12,32,128]{2,1,0:T(8,128)(2,1)S(1)} %get-tuple-element.68.b_ref), channel_id=1, source_target_pairs={{1,0},{2,1},{3,2},{4,3},{5,4},{6,5},{7,6},{0,7},{9,8},{10,9},{11,1... | collective-permute-start | bytes 294920 | tf_op jit(solution)/shard_map/ppermute | solution.py:57
  202.0 3.3 %collective-permute-done.30.a_ref = bf16[12,32,128]{2,1,0:T(8,128)(2,1)S(1)} collective-permute-done((bf16[12,32,128]{2,1,0:T(8,128)(2,1)S(1)}, bf16[12,32,128]{2,1,0:T(8,128)(2,1)S(1)}, u32[]{:S(2)}, u32[]{:S(2)}) %collective-permute-start.30) | collective-permute-done | bytes 98336 | tf_op jit(solution)/shard_map/ppermute | solution.py:57
  205.3 3.2 %shard_map.172 = (f32[12,32,128]{2,1,0:T(8,128)}, bf16[12,32,128]{2,1,0:T(8,128)(2,1)S(1)}) custom-call(s32[60]{0:T(128)S(1)} %reshape.27.cols_ref, bf16[12,32,128]{2,1,0:T(8,128)(2,1)S(1)} %collective-permute-done.30.a_ref, bf16[12,32,128]{2,1,0:T(8,128)(2,1)S(1)} %get-tuple-element.68.b_ref, bf16[12,32,128]{2,1,0:T(8,128)(2,1)S(1)} %collective-permute-done.31.c_ref, ...), custom_call_target="tpu_custom_call" | custom-call | tf_op jit(solution)/shard_map/pallas_call | solution.py:271
  208.8 4.9 %collective-permute-start.34 = (bf16[12,32,128]{2,1,0:T(8,128)(2,1)S(1)}, bf16[12,32,128]{2,1,0:T(8,128)(2,1)S(1)}, u32[]{:S(2)}, u32[]{:S(2)}) collective-permute-start(bf16[12,32,128]{2,1,0:T(8,128)(2,1)S(1)} %get-tuple-element.70.refs_1_), channel_id=1, source_target_pairs={{0,3},{1,4},{2,5},{3,6},{4,7},{5,0},{6,1},{7,2},{8,11},{9,12},{10,... | collective-permute-start | bytes 294920 | tf_op jit(solution)/shard_map/ppermute | solution.py:412
  214.7 3.8 %collective-permute-start.36 = (bf16[12,32,128]{2,1,0:T(8,128)(2,1)S(1)}, bf16[12,32,128]{2,1,0:T(8,128)(2,1)S(1)}, u32[]{:S(2)}, u32[]{:S(2)}) collective-permute-start(bf16[12,32,128]{2,1,0:T(8,128)(2,1)S(1)} %get-tuple-element.70.refs_1_), channel_id=1, source_target_pairs={{0,5},{1,6},{2,7},{3,0},{4,1},{5,2},{6,3},{7,4},{8,13},{9,14},{10,... | collective-permute-start | bytes 294920 | tf_op jit(solution)/shard_map/ppermute | solution.py:412
  220.4 4.6 %collective-permute-done.34.refs_4_ = bf16[12,32,128]{2,1,0:T(8,128)(2,1)S(1)} collective-permute-done((bf16[12,32,128]{2,1,0:T(8,128)(2,1)S(1)}, bf16[12,32,128]{2,1,0:T(8,128)(2,1)S(1)}, u32[]{:S(2)}, u32[]{:S(2)}) %collective-permute-start.34) | collective-permute-done | bytes 98336 | tf_op jit(solution)/shard_map/ppermute | solution.py:412
  225.5 11.6 %shard_map.173 = f32[48,32,128]{2,1,0:T(8,128)} custom-call(s32[240]{0:T(256)S(1)} %reshape.25.cols_ref, s32[144]{0:T(256)S(1)} %pad_add_fusion.2.to_ref, s32[8]{0:T(128)S(1)} %and_select_fusion.3.order_ref, s32[144,128]{1,0:T(8,128)S(1)} %pad_add_fusion.refs_0_, bf16[12,32,128]{2,1,0:T(8,128)(2,1)S(1)} %get-tuple-element.70.refs_1_, ...), custom_call_target="tpu_custom_call" | custom-call | tf_op jit(solution)/shard_map/pallas_call | solution.py:214
  (142 shorter events, 55.0 us)
Async XLA Ops:
  4.7 19.8 %collective-permute-start.2 = (bf16[48,32,128]{2,1,0:T(8,128)(2,1)S(1)}, bf16[48,32,128]{2,1,0:T(8,128)(2,1)}, u32[]{:S(2)}, u32[]{:S(2)}) collective-permute-start(bf16[48,32,128]{2,1,0:T(8,128)(2,1)S(1)} %get-tuple-element.39.b_ref), channel_id=1, source_target_pairs={{0,1},{1,2},{2,3},{3,4},{4,5},{5,6},{6,7},{7,0},{8,9},{9,10},{10,1... | collective-permute-start | bytes 1179656 | tf_op jit(solution)/shard_map/ppermute | solution.py:57
  7.7 19.1 %collective-permute-start.3 = (bf16[48,32,128]{2,1,0:T(8,128)(2,1)S(1)}, bf16[48,32,128]{2,1,0:T(8,128)(2,1)}, u32[]{:S(2)}, u32[]{:S(2)}) collective-permute-start(bf16[48,32,128]{2,1,0:T(8,128)(2,1)S(1)} %get-tuple-element.39.b_ref), channel_id=1, source_target_pairs={{1,0},{2,1},{3,2},{4,3},{5,4},{6,5},{7,6},{0,7},{9,8},{10,9},{11,1... | collective-permute-start | bytes 1179656 | tf_op jit(solution)/shard_map/ppermute | solution.py:57
  40.3 16.3 %collective-permute-start.4 = (bf16[48,32,128]{2,1,0:T(8,128)(2,1)S(1)}, bf16[48,32,128]{2,1,0:T(8,128)(2,1)S(1)}, u32[]{:S(2)}, u32[]{:S(2)}) collective-permute-start(bf16[48,32,128]{2,1,0:T(8,128)(2,1)S(1)} %get-tuple-element.41.b_ref), channel_id=1, source_target_pairs={{0,1},{1,2},{2,3},{3,4},{4,5},{5,6},{6,7},{7,0},{8,9},{9,10},{10,1... | collective-permute-start | bytes 1179656 | tf_op jit(solution)/shard_map/ppermute | solution.py:57
  40.6 19.9 %collective-permute-start.5 = (bf16[48,32,128]{2,1,0:T(8,128)(2,1)S(1)}, bf16[48,32,128]{2,1,0:T(8,128)(2,1)S(1)}, u32[]{:S(2)}, u32[]{:S(2)}) collective-permute-start(bf16[48,32,128]{2,1,0:T(8,128)(2,1)S(1)} %get-tuple-element.41.b_ref), channel_id=1, source_target_pairs={{1,0},{2,1},{3,2},{4,3},{5,4},{6,5},{7,6},{0,7},{9,8},{10,9},{11,1... | collective-permute-start | bytes 1179656 | tf_op jit(solution)/shard_map/ppermute | solution.py:57
  71.3 24.7 %all-to-all-start = ((bf16[8,12,32,128]{3,2,1,0:T(8,128)(2,1)}), bf16[8,12,32,128]{3,2,1,0:T(8,128)(2,1)}, u32[]{:S(2)}, u32[]{:S(2)}) async-start(bf16[8,12,32,128]{3,2,1,0:T(8,128)(2,1)} %bitcast.3), calls=%async_computation | async-start | bytes 1572864 | tf_op jit(solution)/shard_map/all_to_all | solution.py:385
  97.6 7.3 %collective-permute-start.6 = (bf16[12,32,128]{2,1,0:T(8,128)(2,1)S(1)}, bf16[12,32,128]{2,1,0:T(8,128)(2,1)S(1)}, u32[]{:S(2)}, u32[]{:S(2)}) collective-permute-start(bf16[12,32,128]{2,1,0:T(8,128)(2,1)S(1)} %get-tuple-element.43.b_ref), channel_id=1, source_target_pairs={{0,1},{1,2},{2,3},{3,4},{4,5},{5,6},{6,7},{7,0},{8,9},{9,10},{10,1... | collective-permute-start | bytes 294920 | tf_op jit(solution)/shard_map/ppermute | solution.py:57
  107.5 7.4 %collective-permute-start.8 = (bf16[12,32,128]{2,1,0:T(8,128)(2,1)S(1)}, bf16[12,32,128]{2,1,0:T(8,128)(2,1)S(1)}, u32[]{:S(2)}, u32[]{:S(2)}) collective-permute-start(bf16[12,32,128]{2,1,0:T(8,128)(2,1)S(1)} %get-tuple-element.46.b_ref), channel_id=1, source_target_pairs={{0,1},{1,2},{2,3},{3,4},{4,5},{5,6},{6,7},{7,0},{8,9},{9,10},{10,1... | collective-permute-start | bytes 294920 | tf_op jit(solution)/shard_map/ppermute | solution.py:57
  107.6 7.3 %collective-permute-start.9 = (bf16[12,32,128]{2,1,0:T(8,128)(2,1)S(1)}, bf16[12,32,128]{2,1,0:T(8,128)(2,1)S(1)}, u32[]{:S(2)}, u32[]{:S(2)}) collective-permute-start(bf16[12,32,128]{2,1,0:T(8,128)(2,1)S(1)} %get-tuple-element.46.b_ref), channel_id=1, source_target_pairs={{1,0},{2,1},{3,2},{4,3},{5,4},{6,5},{7,6},{0,7},{9,8},{10,9},{11,1... | collective-permute-start | bytes 294920 | tf_op jit(solution)/shard_map/ppermute | solution.py:57
  122.3 6.8 %collective-permute-start.13 = (bf16[12,8,128]{2,1,0:T(8,128)(2,1)S(1)}, bf16[12,8,128]{2,1,0:T(8,128)(2,1)S(1)}, u32[]{:S(2)}, u32[]{:S(2)}) collective-permute-start(bf16[12,8,128]{2,1,0:T(8,128)(2,1)S(1)} %get-tuple-element.51.b_ref), channel_id=1, source_target_pairs={{0,1},{1,2},{2,3},{3,4},{4,5},{5,6},{6,7},{7,0},{8,9},{9,10},{10,1... | collective-permute-start | bytes 73736 | tf_op jit(solution)/shard_map/ppermute | solution.py:57
  122.3 6.8 %collective-permute-start.14 = (bf16[12,8,128]{2,1,0:T(8,128)(2,1)S(1)}, bf16[12,8,128]{2,1,0:T(8,128)(2,1)S(1)}, u32[]{:S(2)}, u32[]{:S(2)}) collective-permute-start(bf16[12,8,128]{2,1,0:T(8,128)(2,1)S(1)} %get-tuple-element.51.b_ref), channel_id=1, source_target_pairs={{1,0},{2,1},{3,2},{4,3},{5,4},{6,5},{7,6},{0,7},{9,8},{10,9},{11,1... | collective-permute-start | bytes 73736 | tf_op jit(solution)/shard_map/ppermute | solution.py:57
  132.3 6.6 %collective-permute-start.15 = (bf16[12,8,128]{2,1,0:T(8,128)(2,1)S(1)}, bf16[12,8,128]{2,1,0:T(8,128)(2,1)S(1)}, u32[]{:S(2)}, u32[]{:S(2)}) collective-permute-start(bf16[12,8,128]{2,1,0:T(8,128)(2,1)S(1)} %get-tuple-element.54.b_ref), channel_id=1, source_target_pairs={{0,1},{1,2},{2,3},{3,4},{4,5},{5,6},{6,7},{7,0},{8,9},{9,10},{10,1... | collective-permute-start | bytes 73736 | tf_op jit(solution)/shard_map/ppermute | solution.py:57
  132.3 6.6 %collective-permute-start.16 = (bf16[12,8,128]{2,1,0:T(8,128)(2,1)S(1)}, bf16[12,8,128]{2,1,0:T(8,128)(2,1)S(1)}, u32[]{:S(2)}, u32[]{:S(2)}) collective-permute-start(bf16[12,8,128]{2,1,0:T(8,128)(2,1)S(1)} %get-tuple-element.54.b_ref), channel_id=1, source_target_pairs={{1,0},{2,1},{3,2},{4,3},{5,4},{6,5},{7,6},{0,7},{9,8},{10,9},{11,1... | collective-permute-start | bytes 73736 | tf_op jit(solution)/shard_map/ppermute | solution.py:57
  142.1 6.6 %collective-permute-start.17 = (bf16[12,8,128]{2,1,0:T(8,128)(2,1)S(1)}, bf16[12,8,128]{2,1,0:T(8,128)(2,1)S(1)}, u32[]{:S(2)}, u32[]{:S(2)}) collective-permute-start(bf16[12,8,128]{2,1,0:T(8,128)(2,1)S(1)} %get-tuple-element.56.b_ref), channel_id=1, source_target_pairs={{0,1},{1,2},{2,3},{3,4},{4,5},{5,6},{6,7},{7,0},{8,9},{9,10},{10,1... | collective-permute-start | bytes 73736 | tf_op jit(solution)/shard_map/ppermute | solution.py:57
  142.1 6.6 %collective-permute-start.18 = (bf16[12,8,128]{2,1,0:T(8,128)(2,1)S(1)}, bf16[12,8,128]{2,1,0:T(8,128)(2,1)S(1)}, u32[]{:S(2)}, u32[]{:S(2)}) collective-permute-start(bf16[12,8,128]{2,1,0:T(8,128)(2,1)S(1)} %get-tuple-element.56.b_ref), channel_id=1, source_target_pairs={{1,0},{2,1},{3,2},{4,3},{5,4},{6,5},{7,6},{0,7},{9,8},{10,9},{11,1... | collective-permute-start | bytes 73736 | tf_op jit(solution)/shard_map/ppermute | solution.py:57
  151.9 6.6 %collective-permute-start.19 = (bf16[12,8,128]{2,1,0:T(8,128)(2,1)S(1)}, bf16[12,8,128]{2,1,0:T(8,128)(2,1)S(1)}, u32[]{:S(2)}, u32[]{:S(2)}) collective-permute-start(bf16[12,8,128]{2,1,0:T(8,128)(2,1)S(1)} %get-tuple-element.58.b_ref), channel_id=1, source_target_pairs={{0,1},{1,2},{2,3},{3,4},{4,5},{5,6},{6,7},{7,0},{8,9},{9,10},{10,1... | collective-permute-start | bytes 73736 | tf_op jit(solution)/shard_map/ppermute | solution.py:57
  151.9 6.6 %collective-permute-start.20 = (bf16[12,8,128]{2,1,0:T(8,128)(2,1)S(1)}, bf16[12,8,128]{2,1,0:T(8,128)(2,1)S(1)}, u32[]{:S(2)}, u32[]{:S(2)}) collective-permute-start(bf16[12,8,128]{2,1,0:T(8,128)(2,1)S(1)} %get-tuple-element.58.b_ref), channel_id=1, source_target_pairs={{1,0},{2,1},{3,2},{4,3},{5,4},{6,5},{7,6},{0,7},{9,8},{10,9},{11,1... | collective-permute-start | bytes 73736 | tf_op jit(solution)/shard_map/ppermute | solution.py:57
  161.7 6.8 %collective-permute-start.21 = (bf16[12,8,128]{2,1,0:T(8,128)(2,1)S(1)}, bf16[12,8,128]{2,1,0:T(8,128)(2,1)S(1)}, u32[]{:S(2)}, u32[]{:S(2)}) collective-permute-start(bf16[12,8,128]{2,1,0:T(8,128)(2,1)S(1)} %get-tuple-element.60.b_ref), channel_id=1, source_target_pairs={{0,1},{1,2},{2,3},{3,4},{4,5},{5,6},{6,7},{7,0},{8,9},{9,10},{10,1... | collective-permute-start | bytes 73736 | tf_op jit(solution)/shard_map/ppermute | solution.py:57
  161.7 6.8 %collective-permute-start.22 = (bf16[12,8,128]{2,1,0:T(8,128)(2,1)S(1)}, bf16[12,8,128]{2,1,0:T(8,128)(2,1)S(1)}, u32[]{:S(2)}, u32[]{:S(2)}) collective-permute-start(bf16[12,8,128]{2,1,0:T(8,128)(2,1)S(1)} %get-tuple-element.60.b_ref), channel_id=1, source_target_pairs={{1,0},{2,1},{3,2},{4,3},{5,4},{6,5},{7,6},{0,7},{9,8},{10,9},{11,1... | collective-permute-start | bytes 73736 | tf_op jit(solution)/shard_map/ppermute | solution.py:57
  166.5 27.8 %collective-permute-start.1 = (s32[49,128]{1,0:T(8,128)S(1)}, s32[49,128]{1,0:T(8,128)S(1)}, u32[]{:S(2)}, u32[]{:S(2)}) collective-permute-start(s32[49,128]{1,0:T(8,128)S(1)} %pad_add_fusion.1), channel_id=1, source_target_pairs={{1,0},{2,1},{3,2},{4,3},{5,4},{6,5},{7,6},{0,7},{9,8},{10,9},{11,1... | collective-permute-start | bytes 75272 | tf_op jit(solution)/shard_map/ppermute | solution.py:57
  168.5 33.5 %collective-permute-start = (s32[49,128]{1,0:T(8,128)S(1)}, s32[49,128]{1,0:T(8,128)S(1)}, u32[]{:S(2)}, u32[]{:S(2)}) collective-permute-start(s32[49,128]{1,0:T(8,128)S(1)} %pad_add_fusion.1), channel_id=1, source_target_pairs={{0,1},{1,2},{2,3},{3,4},{4,5},{5,6},{6,7},{7,0},{8,9},{9,10},{10,1... | collective-permute-start | bytes 75272 | tf_op jit(solution)/shard_map/ppermute | solution.py:57
  171.8 6.6 %collective-permute-start.23 = (bf16[12,8,128]{2,1,0:T(8,128)(2,1)S(1)}, bf16[12,8,128]{2,1,0:T(8,128)(2,1)S(1)}, u32[]{:S(2)}, u32[]{:S(2)}) collective-permute-start(bf16[12,8,128]{2,1,0:T(8,128)(2,1)S(1)} %get-tuple-element.62.b_ref), channel_id=1, source_target_pairs={{0,1},{1,2},{2,3},{3,4},{4,5},{5,6},{6,7},{7,0},{8,9},{9,10},{10,1... | collective-permute-start | bytes 73736 | tf_op jit(solution)/shard_map/ppermute | solution.py:57
  181.6 6.6 %collective-permute-start.25 = (bf16[12,8,128]{2,1,0:T(8,128)(2,1)S(1)}, bf16[12,8,128]{2,1,0:T(8,128)(2,1)S(1)}, u32[]{:S(2)}, u32[]{:S(2)}) collective-permute-start(bf16[12,8,128]{2,1,0:T(8,128)(2,1)S(1)} %get-tuple-element.64.b_ref), channel_id=1, source_target_pairs={{0,1},{1,2},{2,3},{3,4},{4,5},{5,6},{6,7},{7,0},{8,9},{9,10},{10,1... | collective-permute-start | bytes 73736 | tf_op jit(solution)/shard_map/ppermute | solution.py:57
  181.6 6.6 %collective-permute-start.26 = (bf16[12,8,128]{2,1,0:T(8,128)(2,1)S(1)}, bf16[12,8,128]{2,1,0:T(8,128)(2,1)S(1)}, u32[]{:S(2)}, u32[]{:S(2)}) collective-permute-start(bf16[12,8,128]{2,1,0:T(8,128)(2,1)S(1)} %get-tuple-element.64.b_ref), channel_id=1, source_target_pairs={{1,0},{2,1},{3,2},{4,3},{5,4},{6,5},{7,6},{0,7},{9,8},{10,9},{11,1... | collective-permute-start | bytes 73736 | tf_op jit(solution)/shard_map/ppermute | solution.py:57
  197.3 8.0 %collective-permute-start.30 = (bf16[12,32,128]{2,1,0:T(8,128)(2,1)S(1)}, bf16[12,32,128]{2,1,0:T(8,128)(2,1)S(1)}, u32[]{:S(2)}, u32[]{:S(2)}) collective-permute-start(bf16[12,32,128]{2,1,0:T(8,128)(2,1)S(1)} %get-tuple-element.68.b_ref), channel_id=1, source_target_pairs={{0,1},{1,2},{2,3},{3,4},{4,5},{5,6},{6,7},{7,0},{8,9},{9,10},{10,1... | collective-permute-start | bytes 294920 | tf_op jit(solution)/shard_map/ppermute | solution.py:57
  197.3 8.0 %collective-permute-start.31 = (bf16[12,32,128]{2,1,0:T(8,128)(2,1)S(1)}, bf16[12,32,128]{2,1,0:T(8,128)(2,1)S(1)}, u32[]{:S(2)}, u32[]{:S(2)}) collective-permute-start(bf16[12,32,128]{2,1,0:T(8,128)(2,1)S(1)} %get-tuple-element.68.b_ref), channel_id=1, source_target_pairs={{1,0},{2,1},{3,2},{4,3},{5,4},{6,5},{7,6},{0,7},{9,8},{10,9},{11,1... | collective-permute-start | bytes 294920 | tf_op jit(solution)/shard_map/ppermute | solution.py:57
  208.5 9.9 %collective-permute-start.32 = (bf16[12,32,128]{2,1,0:T(8,128)(2,1)S(1)}, bf16[12,32,128]{2,1,0:T(8,128)(2,1)S(1)}, u32[]{:S(2)}, u32[]{:S(2)}) collective-permute-start(bf16[12,32,128]{2,1,0:T(8,128)(2,1)S(1)} %get-tuple-element.70.refs_1_), channel_id=1, source_target_pairs={{0,1},{1,2},{2,3},{3,4},{4,5},{5,6},{6,7},{7,0},{8,9},{9,10},{10,1... | collective-permute-start | bytes 294920 | tf_op jit(solution)/shard_map/ppermute | solution.py:412
  208.5 9.9 %collective-permute-start.33 = (bf16[12,32,128]{2,1,0:T(8,128)(2,1)S(1)}, bf16[12,32,128]{2,1,0:T(8,128)(2,1)S(1)}, u32[]{:S(2)}, u32[]{:S(2)}) collective-permute-start(bf16[12,32,128]{2,1,0:T(8,128)(2,1)S(1)} %get-tuple-element.70.refs_1_), channel_id=1, source_target_pairs={{0,2},{1,3},{2,4},{3,5},{4,6},{5,7},{6,0},{7,1},{8,10},{9,11},{10,... | collective-permute-start | bytes 294920 | tf_op jit(solution)/shard_map/ppermute | solution.py:412
  208.8 16.2 %collective-permute-start.34 = (bf16[12,32,128]{2,1,0:T(8,128)(2,1)S(1)}, bf16[12,32,128]{2,1,0:T(8,128)(2,1)S(1)}, u32[]{:S(2)}, u32[]{:S(2)}) collective-permute-start(bf16[12,32,128]{2,1,0:T(8,128)(2,1)S(1)} %get-tuple-element.70.refs_1_), channel_id=1, source_target_pairs={{0,3},{1,4},{2,5},{3,6},{4,7},{5,0},{6,1},{7,2},{8,11},{9,12},{10,... | collective-permute-start | bytes 294920 | tf_op jit(solution)/shard_map/ppermute | solution.py:412
  213.8 11.6 %collective-permute-start.35 = (bf16[12,32,128]{2,1,0:T(8,128)(2,1)S(1)}, bf16[12,32,128]{2,1,0:T(8,128)(2,1)S(1)}, u32[]{:S(2)}, u32[]{:S(2)}) collective-permute-start(bf16[12,32,128]{2,1,0:T(8,128)(2,1)S(1)} %get-tuple-element.70.refs_1_), channel_id=1, source_target_pairs={{0,4},{1,5},{2,6},{3,7},{4,0},{5,1},{6,2},{7,3},{8,12},{9,13},{10,... | collective-permute-start | bytes 294920 | tf_op jit(solution)/shard_map/ppermute | solution.py:412
  214.7 10.8 %collective-permute-start.36 = (bf16[12,32,128]{2,1,0:T(8,128)(2,1)S(1)}, bf16[12,32,128]{2,1,0:T(8,128)(2,1)S(1)}, u32[]{:S(2)}, u32[]{:S(2)}) collective-permute-start(bf16[12,32,128]{2,1,0:T(8,128)(2,1)S(1)} %get-tuple-element.70.refs_1_), channel_id=1, source_target_pairs={{0,5},{1,6},{2,7},{3,0},{4,1},{5,2},{6,3},{7,4},{8,13},{9,14},{10,... | collective-permute-start | bytes 294920 | tf_op jit(solution)/shard_map/ppermute | solution.py:412
  218.4 7.0 %collective-permute-start.37 = (bf16[12,32,128]{2,1,0:T(8,128)(2,1)S(1)}, bf16[12,32,128]{2,1,0:T(8,128)(2,1)S(1)}, u32[]{:S(2)}, u32[]{:S(2)}) collective-permute-start(bf16[12,32,128]{2,1,0:T(8,128)(2,1)S(1)} %get-tuple-element.70.refs_1_), channel_id=1, source_target_pairs={{0,6},{1,7},{2,0},{3,1},{4,2},{5,3},{6,4},{7,5},{8,14},{9,15},{10,... | collective-permute-start | bytes 294920 | tf_op jit(solution)/shard_map/ppermute | solution.py:412
  218.4 7.0 %collective-permute-start.38 = (bf16[12,32,128]{2,1,0:T(8,128)(2,1)S(1)}, bf16[12,32,128]{2,1,0:T(8,128)(2,1)S(1)}, u32[]{:S(2)}, u32[]{:S(2)}) collective-permute-start(bf16[12,32,128]{2,1,0:T(8,128)(2,1)S(1)} %get-tuple-element.70.refs_1_), channel_id=1, source_target_pairs={{0,7},{1,0},{2,1},{3,2},{4,3},{5,4},{6,5},{7,6},{8,15},{9,8},{10,9... | collective-permute-start | bytes 294920 | tf_op jit(solution)/shard_map/ppermute | solution.py:412
  (35 other events, 711.3 us)
